TPU v7x, 32 devices: a whole 2x2x4 slice. The times are simulated.
32 devices in a mesh: dp: 2 (over core), seq: 16 (over z, y, x).
Axes of the slice: x: 2, y: 2, z: 4, core: 2. Of those that a mesh axis runs over, the one named last changes fastest.
Arguments:
- value_branch: bfloat16 [512, 4096], P(None, ('dp', 'seq')), parts along dimension 1, may hold values from -6 to 6
- first_gate: bfloat16 [512, 4096], P(None, ('dp', 'seq')), parts along dimension 1, may hold values from -6 to 6
- second_gate: bfloat16 [512, 4096], P(None, ('dp', 'seq')), parts along dimension 1, may hold values from -6 to 6
- out_cotangent: bfloat16 [512, 4096], P(None, ('dp', 'seq')), parts along dimension 1, may hold values from -6 to 6
- pos_weight: float32 [64, 33], replicated, may hold values from -4 to 4
- pos_bias: float32 [64], replicated, may hold values from -3.140625 to 3.140625
- mid_weight: float32 [64, 64], replicated, may hold values from -0.75 to 0.75
- mid_bias: float32 [64], replicated, may hold values from -3.140625 to 3.140625
- out_weight: float32 [1024, 64], replicated, may hold values from -0.046875 to 0.046875
- decay_rates: float32 [1024], replicated, may hold values from 3.07 to 15.35
Outputs:
- value_grad: bfloat16 [512, 4096], P(None, ('dp', 'seq')), parts along dimension 1
- first_gate_grad: bfloat16 [512, 4096], P(None, ('dp', 'seq')), parts along dimension 1
- second_gate_grad: bfloat16 [512, 4096], P(None, ('dp', 'seq')), parts along dimension 1
- pos_weight_grad: float32 [128, 33], P('dp'), parts along dimension 0
- pos_bias_grad: float32 [128], P('dp'), parts along dimension 0
- mid_weight_grad: float32 [128, 64], P('dp'), parts along dimension 0
- mid_bias_grad: float32 [128], P('dp'), parts along dimension 0
- out_weight_grad: float32 [1024, 128], P('seq', 'dp'), parts along dimension 1
There are 2 independent parts, one for each index of `dp`. A program takes and returns all parts, laid end to end along the dimension named above; an argument that names none is the same for every part. Nothing has to cross between parts.
All inputs are finite; a program needn't handle non-finite values.
Results may differ from a plain program's by a relative error of at most 0.017.
Values may be sent and summed in bfloat16 or wider, within the bound.
A program may use at most 64 MiB of HBM per device.

v0:
```python
import math

import jax
import jax.numpy as jnp
from jax import lax
from jax.sharding import PartitionSpec as P

RADIX = 128


def make_tables(freq_rows, radix):
    length_all = freq_rows * radix
    freq_index = jnp.arange(freq_rows, dtype=jnp.int32)
    half_index = jnp.arange(freq_rows // 2, dtype=jnp.int32)
    inner_index = jnp.arange(radix, dtype=jnp.int32)
    angle_one = (freq_index[:, None] * half_index[None, :] % freq_rows).astype(jnp.float32) * (
        2.0 * math.pi / freq_rows
    )
    angle_two = (inner_index[:, None] * inner_index[None, :] % radix).astype(jnp.float32) * (
        2.0 * math.pi / radix
    )
    angle_twid = (freq_index[:, None] * inner_index[None, :] % length_all).astype(jnp.float32) * (
        2.0 * math.pi / length_all
    )
    cos_one = jnp.cos(angle_one).astype(jnp.bfloat16)
    sin_one = jnp.sin(angle_one).astype(jnp.bfloat16)
    cos_two = jnp.cos(angle_two).astype(jnp.bfloat16)
    sin_two = jnp.sin(angle_two).astype(jnp.bfloat16)
    left_table = jnp.concatenate([cos_one, -sin_one], axis=0)
    right_fwd = jnp.concatenate(
        [jnp.concatenate([cos_two, -sin_two], axis=1), jnp.concatenate([sin_two, cos_two], axis=1)],
        axis=0,
    )
    right_inv = jnp.concatenate(
        [jnp.concatenate([cos_two, sin_two], axis=1), jnp.concatenate([-sin_two, cos_two], axis=1)],
        axis=0,
    )
    return (left_table, right_fwd, right_inv, jnp.cos(angle_twid), jnp.sin(angle_twid))


def forward_spectrum(signal, tables, freq_rows, radix):
    left_table, right_fwd, right_inv, twid_cos, twid_sin = tables
    count = signal.shape[0]
    shaped = signal.reshape(count, freq_rows // 2, radix)
    stacked = jnp.einsum("kn,rnm->rkm", left_table, shaped, preferred_element_type=jnp.float32)
    real_a = stacked[:, :freq_rows]
    imag_a = stacked[:, freq_rows:]
    real_b = (real_a * twid_cos + imag_a * twid_sin).astype(jnp.bfloat16)
    imag_b = (imag_a * twid_cos - real_a * twid_sin).astype(jnp.bfloat16)
    joined = jnp.concatenate([real_b, imag_b], axis=2)
    spectrum = jnp.einsum("rkn,nm->rkm", joined, right_fwd, preferred_element_type=jnp.float32)
    return (spectrum[:, :, :radix], spectrum[:, :, radix:])


def inverse_signal(product, tables, freq_rows, radix):
    left_table, right_fwd, right_inv, twid_cos, twid_sin = tables
    real_p, imag_p = product
    joined = jnp.concatenate([real_p, imag_p], axis=2)
    section_q = jnp.einsum("rkn,nm->rkm", joined, right_inv, preferred_element_type=jnp.float32)
    real_q = section_q[:, :, :radix]
    imag_q = section_q[:, :, radix:]
    real_r = (real_q * twid_cos - imag_q * twid_sin).astype(jnp.bfloat16)
    imag_r = (imag_q * twid_cos + real_q * twid_sin).astype(jnp.bfloat16)
    rows_both = jnp.concatenate([real_r, imag_r], axis=1)
    output = jnp.einsum("kn,rkm->rnm", left_table, rows_both, preferred_element_type=jnp.float32)
    count = real_p.shape[0]
    return (output * (1.0 / (freq_rows * radix))).reshape(count, freq_rows // 2 * radix)


def spectral_product(left, right, conj_left, conj_right):
    sign_left = -1.0 if conj_left else 1.0
    sign_right = -1.0 if conj_right else 1.0
    real_part = left[0] * right[0] - sign_left * sign_right * left[1] * right[1]
    imag_part = sign_left * left[1] * right[0] + sign_right * left[0] * right[1]
    return (real_part.astype(jnp.bfloat16), imag_part.astype(jnp.bfloat16))


def positional_features(positions, seq_len, bands):
    band_index = jnp.arange(1, bands + 1, dtype=jnp.int32)
    angles = (band_index[:, None] * positions[None, :] % seq_len).astype(jnp.float32) * (
        2.0 * math.pi / seq_len
    )
    ramp = positions.astype(jnp.float32)[None, :] / seq_len
    return jnp.concatenate([ramp, jnp.cos(angles), jnp.sin(angles)], axis=0)


def filter_network(positions, seq_len, pos_weight, pos_bias, mid_weight, mid_bias):
    bands = (pos_weight.shape[1] - 1) // 2
    features = positional_features(positions, seq_len, bands)
    pre_one = jnp.dot(pos_weight, features, precision=lax.Precision.HIGHEST) + pos_bias[:, None]
    act_one = jnp.sin(pre_one)
    pre_two = jnp.dot(mid_weight, act_one, precision=lax.Precision.HIGHEST) + mid_bias[:, None]
    act_two = jnp.sin(pre_two)
    return (features, pre_one, act_one, pre_two, act_two)


def modulation(rates, positions, seq_len):
    return jnp.exp(-rates[:, None] * positions.astype(jnp.float32)[None, :] / seq_len)


def contract_last(left, right):
    return lax.dot_general(left, right, (((1,), (1,)), ((), ())), precision=lax.Precision.HIGHEST)


def network_backward(act_grad, features, pre_one, act_one, pre_two, mid_weight):
    pre_two_grad = act_grad * jnp.cos(pre_two)
    mid_weight_part = contract_last(pre_two_grad, act_one)
    mid_bias_part = jnp.sum(pre_two_grad, axis=1)
    pre_one_grad = jnp.dot(mid_weight.T, pre_two_grad, precision=lax.Precision.HIGHEST) * jnp.cos(
        pre_one
    )
    pos_weight_part = contract_last(pre_one_grad, features)
    pos_bias_part = jnp.sum(pre_one_grad, axis=1)
    return (pos_weight_part, pos_bias_part, mid_weight_part, mid_bias_part)


def on_device(
    value_branch,
    first_gate,
    second_gate,
    out_cotangent,
    pos_weight,
    pos_bias,
    mid_weight,
    mid_bias,
    out_weight,
    decay_rates,
):
    model_width, tok_dev = value_branch.shape
    devices = lax.axis_size("seq")
    seq_len = tok_dev * devices
    channels = model_width // devices
    my_rank = lax.axis_index("seq")
    freq_rows = 2 * seq_len // RADIX
    tables = make_tables(freq_rows, RADIX)
    all_positions = jnp.arange(seq_len, dtype=jnp.int32)
    own_rates = lax.dynamic_slice_in_dim(decay_rates, my_rank * 2 * channels, 2 * channels)
    window_own = modulation(own_rates, all_positions, seq_len)
    value_ch, first_ch = (
        lax.all_to_all(value_branch, "seq", split_axis=0, concat_axis=1, tiled=True),
        lax.all_to_all(first_gate, "seq", split_axis=0, concat_axis=1, tiled=True),
    )
    local_positions = my_rank * tok_dev + jnp.arange(tok_dev, dtype=jnp.int32)
    features, pre_one, act_one, pre_two, act_two = filter_network(
        local_positions, seq_len, pos_weight, pos_bias, mid_weight, mid_bias
    )
    window_local = modulation(decay_rates, local_positions, seq_len)
    local_filters = (
        jnp.dot(out_weight, act_two, precision=lax.Precision.HIGHEST) * window_local
    ).astype(jnp.bfloat16)
    filt_ch = lax.all_to_all(local_filters, "seq", split_axis=0, concat_axis=1, tiled=True)
    filt_real, filt_imag = forward_spectrum(filt_ch, tables, freq_rows, RADIX)
    filt_real = filt_real.reshape(channels, 2, freq_rows, RADIX)
    filt_imag = filt_imag.reshape(channels, 2, freq_rows, RADIX)
    spec_one = (filt_real[:, 0], filt_imag[:, 0])
    spec_two = (filt_real[:, 1], filt_imag[:, 1])
    spec_val = forward_spectrum(value_ch, tables, freq_rows, RADIX)
    conv_one = inverse_signal(
        spectral_product(spec_one, spec_val, False, False), tables, freq_rows, RADIX
    )
    gated = (first_ch.astype(jnp.float32) * conv_one).astype(jnp.bfloat16)
    spec_gated = forward_spectrum(gated, tables, freq_rows, RADIX)
    conv_two = inverse_signal(
        spectral_product(spec_two, spec_gated, False, False), tables, freq_rows, RADIX
    )
    second_ch, cot_ch = (
        lax.all_to_all(second_gate, "seq", split_axis=0, concat_axis=1, tiled=True),
        lax.all_to_all(out_cotangent, "seq", split_axis=0, concat_axis=1, tiled=True),
    )
    cot_wide = cot_ch.astype(jnp.float32)
    second_grad_ch = (cot_wide * conv_two).astype(jnp.bfloat16)
    second_out = lax.all_to_all(second_grad_ch, "seq", split_axis=1, concat_axis=0, tiled=True)
    grad_two = (cot_wide * second_ch.astype(jnp.float32)).astype(jnp.bfloat16)
    spec_gtwo = forward_spectrum(grad_two, tables, freq_rows, RADIX)
    gated_grad = inverse_signal(
        spectral_product(spec_two, spec_gtwo, True, False), tables, freq_rows, RADIX
    )
    filt_grad_two = inverse_signal(
        spectral_product(spec_gtwo, spec_gated, False, True), tables, freq_rows, RADIX
    )
    first_grad_ch = (gated_grad * conv_one).astype(jnp.bfloat16)
    grad_one = (gated_grad * first_ch.astype(jnp.float32)).astype(jnp.bfloat16)
    spec_gone = forward_spectrum(grad_one, tables, freq_rows, RADIX)
    value_grad_ch = inverse_signal(
        spectral_product(spec_one, spec_gone, True, False), tables, freq_rows, RADIX
    ).astype(jnp.bfloat16)
    filt_grad_one = inverse_signal(
        spectral_product(spec_gone, spec_val, False, True), tables, freq_rows, RADIX
    )
    value_out, first_out = (
        lax.all_to_all(value_grad_ch, "seq", split_axis=1, concat_axis=0, tiled=True),
        lax.all_to_all(first_grad_ch, "seq", split_axis=1, concat_axis=0, tiled=True),
    )
    filt_grads = jnp.stack([filt_grad_one, filt_grad_two], axis=1).reshape(2 * channels, seq_len)
    filter_grad_ch = filt_grads * window_own / seq_len
    filter_grad_seq = lax.all_to_all(
        filter_grad_ch.astype(jnp.bfloat16), "seq", split_axis=1, concat_axis=0, tiled=True
    ).astype(filter_grad_ch.dtype)
    out_weight_grad = lax.psum_scatter(
        contract_last(filter_grad_seq, act_two), "seq", scatter_dimension=0, tiled=True
    )
    act_grad = jnp.dot(out_weight.T, filter_grad_seq, precision=lax.Precision.HIGHEST)
    partials = network_backward(act_grad, features, pre_one, act_one, pre_two, mid_weight)
    pos_weight_grad, pos_bias_grad, mid_weight_grad, mid_bias_grad = lax.psum(
        (partials[0], partials[1], partials[2], partials[3]), "seq"
    )
    return (
        value_out,
        first_out,
        second_out,
        pos_weight_grad,
        pos_bias_grad,
        mid_weight_grad,
        mid_bias_grad,
        out_weight_grad,
    )


def solution(mesh):
    in_specs = (
        P(None, ("dp", "seq")),
        P(None, ("dp", "seq")),
        P(None, ("dp", "seq")),
        P(None, ("dp", "seq")),
        P(),
        P(),
        P(),
        P(),
        P(),
        P(),
    )
    out_specs = (
        P(None, ("dp", "seq")),
        P(None, ("dp", "seq")),
        P(None, ("dp", "seq")),
        P("dp", None),
        P("dp"),
        P("dp", None),
        P("dp"),
        P("seq", "dp"),
    )
    return jax.shard_map(
        on_device, mesh=mesh, in_specs=in_specs, out_specs=out_specs, check_vma=False
    )
```

profile of v0, /device:TPU:0, one launch (start us, length us, event | category | flops | bytes accessed | tf_op | source)
XLA Modules:
  0.0 213.4 jit_solution(16304408818487413228)
XLA Ops:
  7.2 8.5 %all-to-all-start.1 = ((bf16[16,32,128]{2,1,0:T(8,128)(2,1)}), bf16[16,32,128]{2,1,0:T(8,128)(2,1)S(1)}, u32[]{:S(2)}, u32[]{:S(2)}) async-start(bf16[16,32,128]{2,1,0:T(8,128)(2,1)} %bitcast.178), calls=%async_computation.1 | async-start | bytes 262144 | tf_op jit(solution)/shard_map/all_to_all | solution.py:168
  16.0 1.6 fusion.149
  17.7 1.6 fusion.150
  20.7 2.8 %all-to-all-done.1 = bf16[16,32,128]{2,1,0:T(8,128)(2,1)S(1)} async-done(((bf16[16,32,128]{2,1,0:T(8,128)(2,1)}), bf16[16,32,128]{2,1,0:T(8,128)(2,1)S(1)}, u32[]{:S(2)}, u32[]{:S(2)}) %all-to-all-start.1) | async-done | bytes 131104 | tf_op jit(solution)/shard_map/all_to_all | solution.py:168
  23.4 4.2 %all-to-all-start.5 = ((bf16[16,32,128]{2,1,0:T(8,128)(2,1)}), bf16[16,32,128]{2,1,0:T(8,128)(2,1)S(1)}, u32[]{:S(2)}, u32[]{:S(2)}) async-start(bf16[16,32,128]{2,1,0:T(8,128)(2,1)} %bitcast.179), calls=%async_computation.5 | async-start | bytes 262144 | tf_op jit(solution)/shard_map/all_to_all | solution.py:140
  29.1 6.3 %all-to-all-done.5 = bf16[16,32,128]{2,1,0:T(8,128)(2,1)S(1)} async-done(((bf16[16,32,128]{2,1,0:T(8,128)(2,1)}), bf16[16,32,128]{2,1,0:T(8,128)(2,1)S(1)}, u32[]{:S(2)}, u32[]{:S(2)}) %all-to-all-start.5) | async-done | bytes 131104 | tf_op jit(solution)/shard_map/all_to_all | solution.py:140
  35.4 3.5 %all-to-all-start.2 = ((bf16[16,32,128]{2,1,0:T(8,128)(2,1)}), bf16[16,32,128]{2,1,0:T(8,128)(2,1)S(1)}, u32[]{:S(2)}, u32[]{:S(2)}) async-start(bf16[16,32,128]{2,1,0:T(8,128)(2,1)} %bitcast.11), calls=%async_computation.2 | async-start | bytes 262144 | tf_op jit(solution)/shard_map/all_to_all | solution.py:167
  39.3 7.4 %all-to-all-done.2 = bf16[16,32,128]{2,1,0:T(8,128)(2,1)S(1)} async-done(((bf16[16,32,128]{2,1,0:T(8,128)(2,1)}), bf16[16,32,128]{2,1,0:T(8,128)(2,1)S(1)}, u32[]{:S(2)}, u32[]{:S(2)}) %all-to-all-start.2) | async-done | bytes 131104 | tf_op jit(solution)/shard_map/all_to_all | solution.py:167
  46.7 4.2 %all-to-all-start = ((bf16[16,64,128]{2,1,0:T(8,128)(2,1)}), bf16[16,64,128]{2,1,0:T(8,128)(2,1)}, u32[]{:S(2)}, u32[]{:S(2)}) async-start(bf16[16,64,128]{2,1,0:T(8,128)(2,1)} %bitcast.1), calls=%async_computation | async-start | bytes 524288 | tf_op jit(solution)/shard_map/all_to_all | solution.py:151
  52.2 7.3 %all-to-all-done = bf16[16,64,128]{2,1,0:T(8,128)(2,1)} async-done(((bf16[16,64,128]{2,1,0:T(8,128)(2,1)}), bf16[16,64,128]{2,1,0:T(8,128)(2,1)}, u32[]{:S(2)}, u32[]{:S(2)}) %all-to-all-start) | async-done | bytes 262176 | tf_op jit(solution)/shard_map/all_to_all | solution.py:151
  59.4 4.2 %all-to-all-start.3 = ((bf16[16,32,128]{2,1,0:T(8,128)(2,1)}), bf16[16,32,128]{2,1,0:T(8,128)(2,1)}, u32[]{:S(2)}, u32[]{:S(2)}) async-start(bf16[16,32,128]{2,1,0:T(8,128)(2,1)} %bitcast.18), calls=%async_computation.3 | async-start | bytes 262144 | tf_op jit(solution)/shard_map/all_to_all | solution.py:141
  63.6 1.4 convolution_bitcast_fusion
  69.6 1.8 all-to-all-done.3
  71.4 1.4 convolution_bitcast_fusion.1
  74.9 1.3 convolution_bitcast_fusion.3
  80.3 5.0 %all-to-all-start.7 = ((bf16[32,16,128]{2,0,1:T(8,128)(2,1)}), bf16[32,16,128]{2,0,1:T(8,128)(2,1)S(1)}, u32[]{:S(2)}, u32[]{:S(2)}) async-start(bf16[32,16,128]{2,0,1:T(8,128)(2,1)} %copy.51), calls=%async_computation.7 | async-start | bytes 262144 | tf_op jit(solution)/shard_map/all_to_all | solution.py:172
  87.0 6.1 %all-to-all-done.7 = bf16[32,16,128]{2,0,1:T(8,128)(2,1)S(1)} async-done(((bf16[32,16,128]{2,0,1:T(8,128)(2,1)}), bf16[32,16,128]{2,0,1:T(8,128)(2,1)S(1)}, u32[]{:S(2)}, u32[]{:S(2)}) %all-to-all-start.7) | async-done | bytes 131104 | tf_op jit(solution)/shard_map/all_to_all | solution.py:172
  93.1 3.5 %all-to-all-start.4 = ((bf16[32,16,128]{2,0,1:T(8,128)(2,1)}), bf16[32,16,128]{2,0,1:T(8,128)(2,1)S(1)}, u32[]{:S(2)}, u32[]{:S(2)}) async-start(bf16[32,16,128]{2,0,1:T(8,128)(2,1)} %copy.48), calls=%async_computation.4 | async-start | bytes 262144 | tf_op jit(solution)/shard_map/all_to_all | solution.py:191
  97.7 6.7 %all-to-all-done.4 = bf16[32,16,128]{2,0,1:T(8,128)(2,1)S(1)} async-done(((bf16[32,16,128]{2,0,1:T(8,128)(2,1)}), bf16[32,16,128]{2,0,1:T(8,128)(2,1)S(1)}, u32[]{:S(2)}, u32[]{:S(2)}) %all-to-all-start.4) | async-done | bytes 131104 | tf_op jit(solution)/shard_map/all_to_all | solution.py:191
  104.5 3.7 %all-to-all-start.6 = ((bf16[32,16,128]{2,0,1:T(8,128)(2,1)}), bf16[32,16,128]{2,0,1:T(8,128)(2,1)S(1)}, u32[]{:S(2)}, u32[]{:S(2)}) async-start(bf16[32,16,128]{2,0,1:T(8,128)(2,1)} %copy.50), calls=%async_computation.6 | async-start | bytes 262144 | tf_op jit(solution)/shard_map/all_to_all | solution.py:192
  110.1 5.6 %all-to-all-done.6 = bf16[32,16,128]{2,0,1:T(8,128)(2,1)S(1)} async-done(((bf16[32,16,128]{2,0,1:T(8,128)(2,1)}), bf16[32,16,128]{2,0,1:T(8,128)(2,1)S(1)}, u32[]{:S(2)}, u32[]{:S(2)}) %all-to-all-start.6) | async-done | bytes 131104 | tf_op jit(solution)/shard_map/all_to_all | solution.py:192
  115.8 3.5 %all-to-all-start.8 = ((bf16[64,16,128]{2,0,1:T(8,128)(2,1)}), bf16[64,16,128]{2,0,1:T(8,128)(2,1)S(1)}, u32[]{:S(2)}, u32[]{:S(2)}) async-start(bf16[64,16,128]{2,0,1:T(8,128)(2,1)} %copy.54), calls=%async_computation.8 | async-start | bytes 524288 | tf_op jit(solution)/shard_map/all_to_all | solution.py:196
  119.3 8.4 %all-to-all-done.8 = bf16[64,16,128]{2,0,1:T(8,128)(2,1)S(1)} async-done(((bf16[64,16,128]{2,0,1:T(8,128)(2,1)}), bf16[64,16,128]{2,0,1:T(8,128)(2,1)S(1)}, u32[]{:S(2)}, u32[]{:S(2)}) %all-to-all-start.8) | async-done | bytes 262176 | tf_op jit(solution)/shard_map/all_to_all | solution.py:196
  130.1 74.4 %all-reduce = (f32[64,33]{0,1:T(8,128)}, f32[64]{0:T(128)}, f32[64,64]{1,0:T(8,128)}, f32[64]{0:T(128)}) all-reduce(f32[64,33]{0,1:T(8,128)S(1)} %fusion.101, f32[64]{0:T(128)S(1)} %get-tuple-element.70, f32[64,64]{1,0:T(8,128)S(1)} %fusion.153, f32[64]{0:T(128)S(1)} %get-tuple-element.72), channel_id=1, replica_groups=mesh['dp'=2,'seq'=16] {'seq'}, use_global_device_ids=true, to_apply=%region_0.1 | all-reduce | flops 6336 | bytes 50688 | tf_op jit(solution)/shard_map/psum | solution.py:204
  (101 shorter events, 24.2 us)
Async XLA Ops:
  7.2 12.9 %copy-start = (f32[1024,64]{0,1:T(8,128)S(1)}, f32[1024,64]{0,1:T(8,128)}, u32[]{:S(2)}) copy-start(f32[1024,64]{0,1:T(8,128)} %param.18) | copy-start | bytes 786436
  7.2 16.3 %all-to-all-start.1 = ((bf16[16,32,128]{2,1,0:T(8,128)(2,1)}), bf16[16,32,128]{2,1,0:T(8,128)(2,1)S(1)}, u32[]{:S(2)}, u32[]{:S(2)}) async-start(bf16[16,32,128]{2,1,0:T(8,128)(2,1)} %bitcast.178), calls=%async_computation.1 | async-start | bytes 262144 | tf_op jit(solution)/shard_map/all_to_all | solution.py:168
  16.0 1.7 copy-start.14
  17.7 2.4 %copy-start.8 = (f32[128,64]{0,1:T(8,128)}, f32[128,64]{0,1:T(8,128)S(1)}, u32[]{:S(2)}) copy-start(f32[128,64]{0,1:T(8,128)S(1)} %get-tuple-element.64) | copy-start | bytes 98308
  19.3 4.2 %copy-start.10 = (f32[128,64]{0,1:T(8,128)}, f32[128,64]{0,1:T(8,128)S(1)}, u32[]{:S(2)}) copy-start(f32[128,64]{0,1:T(8,128)S(1)} %get-tuple-element.66) | copy-start | bytes 98308
  23.4 27.8 %copy-start.5 = (bf16[16,32,128]{2,1,0:T(8,128)(2,1)}, bf16[16,32,128]{2,1,0:T(8,128)(2,1)S(1)}, u32[]{:S(2)}) copy-start(bf16[16,32,128]{2,1,0:T(8,128)(2,1)S(1)} %all-to-all-done.1) | copy-start | bytes 393220
  23.4 12.0 %all-to-all-start.5 = ((bf16[16,32,128]{2,1,0:T(8,128)(2,1)}), bf16[16,32,128]{2,1,0:T(8,128)(2,1)S(1)}, u32[]{:S(2)}, u32[]{:S(2)}) async-start(bf16[16,32,128]{2,1,0:T(8,128)(2,1)} %bitcast.179), calls=%async_computation.5 | async-start | bytes 262144 | tf_op jit(solution)/shard_map/all_to_all | solution.py:140
  35.4 11.3 %all-to-all-start.2 = ((bf16[16,32,128]{2,1,0:T(8,128)(2,1)}), bf16[16,32,128]{2,1,0:T(8,128)(2,1)S(1)}, u32[]{:S(2)}, u32[]{:S(2)}) async-start(bf16[16,32,128]{2,1,0:T(8,128)(2,1)} %bitcast.11), calls=%async_computation.2 | async-start | bytes 262144 | tf_op jit(solution)/shard_map/all_to_all | solution.py:167
  46.7 12.7 %all-to-all-start = ((bf16[16,64,128]{2,1,0:T(8,128)(2,1)}), bf16[16,64,128]{2,1,0:T(8,128)(2,1)}, u32[]{:S(2)}, u32[]{:S(2)}) async-start(bf16[16,64,128]{2,1,0:T(8,128)(2,1)} %bitcast.1), calls=%async_computation | async-start | bytes 524288 | tf_op jit(solution)/shard_map/all_to_all | solution.py:151
  59.4 12.0 %all-to-all-start.3 = ((bf16[16,32,128]{2,1,0:T(8,128)(2,1)}), bf16[16,32,128]{2,1,0:T(8,128)(2,1)}, u32[]{:S(2)}, u32[]{:S(2)}) async-start(bf16[16,32,128]{2,1,0:T(8,128)(2,1)} %bitcast.18), calls=%async_computation.3 | async-start | bytes 262144 | tf_op jit(solution)/shard_map/all_to_all | solution.py:141
  74.9 1.8 copy-start.2
  79.1 17.7 %copy-start.7 = (bf16[32,16,128]{2,1,0:T(8,128)(2,1)S(1)}, bf16[32,16,128]{2,1,0:T(8,128)(2,1)}, u32[]{:S(2)}) copy-start(bf16[32,16,128]{2,1,0:T(8,128)(2,1)} %get-tuple-element.68) | copy-start | bytes 393220
  80.3 12.8 %all-to-all-start.7 = ((bf16[32,16,128]{2,0,1:T(8,128)(2,1)}), bf16[32,16,128]{2,0,1:T(8,128)(2,1)S(1)}, u32[]{:S(2)}, u32[]{:S(2)}) async-start(bf16[32,16,128]{2,0,1:T(8,128)(2,1)} %copy.51), calls=%async_computation.7 | async-start | bytes 262144 | tf_op jit(solution)/shard_map/all_to_all | solution.py:172
  93.1 11.3 %all-to-all-start.4 = ((bf16[32,16,128]{2,0,1:T(8,128)(2,1)}), bf16[32,16,128]{2,0,1:T(8,128)(2,1)S(1)}, u32[]{:S(2)}, u32[]{:S(2)}) async-start(bf16[32,16,128]{2,0,1:T(8,128)(2,1)} %copy.48), calls=%async_computation.4 | async-start | bytes 262144 | tf_op jit(solution)/shard_map/all_to_all | solution.py:191
  97.7 30.0 %copy-start.11 = (f32[128,64]{0,1:T(8,128)S(1)}, f32[128,64]{0,1:T(8,128)}, u32[]{:S(2)}) copy-start(f32[128,64]{0,1:T(8,128)} %copy-done.10) | copy-start | bytes 98308
  104.5 11.3 %all-to-all-start.6 = ((bf16[32,16,128]{2,0,1:T(8,128)(2,1)}), bf16[32,16,128]{2,0,1:T(8,128)(2,1)S(1)}, u32[]{:S(2)}, u32[]{:S(2)}) async-start(bf16[32,16,128]{2,0,1:T(8,128)(2,1)} %copy.50), calls=%async_computation.6 | async-start | bytes 262144 | tf_op jit(solution)/shard_map/all_to_all | solution.py:192
  108.7 20.3 %copy-start.13 = (f32[128,64]{0,1:T(8,128)S(1)}, f32[128,64]{0,1:T(8,128)}, u32[]{:S(2)}) copy-start(f32[128,64]{0,1:T(8,128)} %get-tuple-element.67) | copy-start | bytes 98308
  109.1 20.3 %copy-start.12 = (f32[64,64]{1,0:T(8,128)S(1)}, f32[64,64]{1,0:T(8,128)}, u32[]{:S(2)}) copy-start(f32[64,64]{1,0:T(8,128)} %param.16) | copy-start | bytes 49156
  109.1 20.3 %copy-start.18 = (f32[128,64]{0,1:T(8,128)S(1)}, f32[128,64]{0,1:T(8,128)}, u32[]{:S(2)}) copy-start(f32[128,64]{0,1:T(8,128)} %get-tuple-element.65) | copy-start | bytes 98308
  109.1 20.6 %copy-start.15 = (f32[16,128]{1,0:T(8,128)S(1)}, f32[16,128]{1,0:T(8,128)}, u32[]{:S(2)}) copy-start(f32[16,128]{1,0:T(8,128)} %copy-done.14) | copy-start | bytes 24580
  109.1 20.6 %copy-start.17 = (f32[16,128]{1,0:T(8,128)S(1)}, f32[16,128]{1,0:T(8,128)}, u32[]{:S(2)}) copy-start(f32[16,128]{1,0:T(8,128)} %copy-done.16) | copy-start | bytes 24580
  109.1 20.8 %copy-start.9 = (f32[128,64]{0,1:T(8,128)S(1)}, f32[128,64]{0,1:T(8,128)}, u32[]{:S(2)}) copy-start(f32[128,64]{0,1:T(8,128)} %copy-done.8) | copy-start | bytes 98308
  115.8 12.0 %all-to-all-start.8 = ((bf16[64,16,128]{2,0,1:T(8,128)(2,1)}), bf16[64,16,128]{2,0,1:T(8,128)(2,1)S(1)}, u32[]{:S(2)}, u32[]{:S(2)}) async-start(bf16[64,16,128]{2,0,1:T(8,128)(2,1)} %copy.54), calls=%async_computation.8 | async-start | bytes 524288 | tf_op jit(solution)/shard_map/all_to_all | solution.py:196
  119.3 85.3 %reduce-scatter.2.cloned.1.call-start = ((), (), s32[]{:S(2)}) async-start(), calls=%async_computation.10 | async-start | bytes 557056 | tf_op jit(solution)/shard_map/reduce_scatter | solution.py:199
  (5 other events, 5.9 us)
Sparse Core Ops, SparseCore 0:
  129.1 74.3 reduce-scatter.1
where the time goes:
time: 215 us; the launch traced here: 213 us
  blocking collectives  74.4 us (35%)
  waiting for transfers between devices  52.5 us (24%)
  starting transfers between devices  40.3 us (19%)
  matrix products  17.9 us (8%)
  between operations  14.5 us (7%)
  local copies, waits for them, and re-layouts  7.72 us (4%)
  other arithmetic  5.94 us (3%)
    psum x1, blocking collectives, on_device(): lax.psum((partials[0], partials[1], partials[2], partials[3]), 'seq')  74.4 us
    all_to_all x1, starting transfers between devices, on_device(): lax.all_to_all(out_cotangent, 'seq', split_axis=0, concat_axis=1, tiled=T...  8.46 us
    all_to_all x1, waiting for transfers between devices, on_device(): lax.all_to_all(filter_grad_ch.astype(jnp.bfloat16), 'seq', split_axis=1,...  8.42 us
    all_to_all x1, waiting for transfers between devices, on_device(): lax.all_to_all(second_gate, 'seq', split_axis=0, concat_axis=1, tiled=True)  7.44 us
    all_to_all x1, waiting for transfers between devices, on_device(): lax.all_to_all(local_filters, 'seq', split_axis=0, concat_axis=1, tiled=T...  7.27 us
    all_to_all x1, waiting for transfers between devices, on_device(): lax.all_to_all(value_grad_ch, 'seq', split_axis=1, concat_axis=0, tiled=T...  6.73 us
    all_to_all x1, waiting for transfers between devices, on_device(): lax.all_to_all(value_branch, 'seq', split_axis=0, concat_axis=1, tiled=True)  6.31 us
    all_to_all x1, waiting for transfers between devices, on_device(): lax.all_to_all(second_grad_ch, 'seq', split_axis=1, concat_axis=0, tiled=...  6.14 us
  transfers between devices with their start and end apart: 10, of which 9 were waited for; matrix products, arithmetic and copies ran while one was open for 9% of the time, Pallas kernels for 0%

commit v1 on v0

--- a/solution.py
+++ b/solution.py
@@ -1,11 +1,19 @@
+import functools
 import math
 
 import jax
 import jax.numpy as jnp
+import ml_dtypes
+import numpy as np
 from jax import lax
+from jax.experimental import pallas as pl
+from jax.experimental.pallas import tpu as pltpu
 from jax.sharding import PartitionSpec as P
 
 RADIX = 128
+GROUP = 16
+MESH = pl.DeviceIdType.MESH
+HIGHEST = lax.Precision.HIGHEST
 
 
 def make_tables(freq_rows, radix):
@@ -114,7 +122,7 @@
     return (pos_weight_part, pos_bias_part, mid_weight_part, mid_bias_part)
 
 
-def on_device(
+def on_device_plain(
     value_branch,
     first_gate,
     second_gate,
@@ -216,6 +224,443 @@
     )
 
 
+def numpy_tables(freq_rows, radix, seq_len, bands, group):
+    half = freq_rows // 2
+    length_all = freq_rows * radix
+    freq_index = np.arange(freq_rows)
+    inner = np.arange(radix)
+    angle_one = (freq_index[:, None] * np.arange(half)[None, :] % freq_rows) * (2.0 * np.pi / freq_rows)
+    angle_two = (inner[:, None] * inner[None, :] % radix) * (2.0 * np.pi / radix)
+    angle_twid = (freq_index[:, None] * inner[None, :] % length_all) * (2.0 * np.pi / length_all)
+    left = np.concatenate([np.cos(angle_one), -np.sin(angle_one)], axis=0)
+    left_fwd = np.kron(left, np.eye(group))
+    left_inv = left_fwd.T / length_all
+    cos_two, sin_two = np.cos(angle_two), np.sin(angle_two)
+    right_fwd = np.block([[cos_two, -sin_two], [sin_two, cos_two]])
+    right_inv = np.block([[cos_two, sin_two], [-sin_two, cos_two]])
+    twid_cos = np.repeat(np.cos(angle_twid), group, axis=0)
+    twid_sin = np.repeat(np.sin(angle_twid), group, axis=0)
+    positions = np.arange(seq_len)
+    band = np.arange(1, bands + 1)
+    angles = (band[:, None] * positions[None, :] % seq_len) * (2.0 * np.pi / seq_len)
+    features = np.zeros((64, seq_len))
+    features[0] = positions / seq_len
+    features[1 : bands + 1] = np.cos(angles)
+    features[bands + 1 : 2 * bands + 1] = np.sin(angles)
+    features[2 * bands + 1] = 1.0
+    low = [table.astype(ml_dtypes.bfloat16) for table in (left_fwd, left_inv, right_fwd, right_inv)]
+    wide = [table.astype(np.float32) for table in (twid_cos, twid_sin, features)]
+    return low + wide
+
+
+def sin_cos(x):
+    turns = jnp.floor(x * (1.0 / math.pi) + 0.5)
+    rest = x - turns * 3.140625
+    rest = rest - turns * 9.67502593994140625e-4
+    rest = rest - turns * 1.509957990978376432e-7
+    sign = 1.0 - 2.0 * (turns - 2.0 * jnp.floor(turns * 0.5))
+    square = rest * rest
+    odd = 1.0 / 6227020800.0
+    for term in (-1.0 / 39916800.0, 1.0 / 362880.0, -1.0 / 5040.0, 1.0 / 120.0, -1.0 / 6.0, 1.0):
+        odd = odd * square + term
+    even = 1.0 / 479001600.0
+    for term in (-1.0 / 3628800.0, 1.0 / 40320.0, -1.0 / 720.0, 1.0 / 24.0, -0.5, 1.0):
+        even = even * square + term
+    return sign * rest * odd, sign * even
+
+
+def wide_dot(left, right):
+    return jnp.dot(left, right, precision=HIGHEST, preferred_element_type=jnp.float32)
+
+
+def short_dot(left, right):
+    return jnp.dot(left, right, preferred_element_type=jnp.float32)
+
+
+def contract_dims(left, right, left_dim, right_dim):
+    return lax.dot_general(
+        left,
+        right,
+        (((left_dim,), (right_dim,)), ((), ())),
+        precision=HIGHEST,
+        preferred_element_type=jnp.float32,
+    )
+
+
+def as_column(row, count):
+    width = row.shape[1]
+    diagonal = lax.broadcasted_iota(jnp.int32, (count, width), 0) == lax.broadcasted_iota(
+        jnp.int32, (count, width), 1
+    )
+    return jnp.sum(jnp.where(diagonal, row, 0.0), axis=1, keepdims=True)
+
+
+def operator_kernel(
+    devices,
+    channels,
+    features_used,
+    value_ref,
+    first_ref,
+    second_ref,
+    cot_ref,
+    pos_weight_ref,
+    pos_bias_ref,
+    mid_weight_ref,
+    mid_bias_ref,
+    out_weight_ref,
+    rates_ref,
+    left_fwd_ref,
+    left_inv_ref,
+    right_fwd_ref,
+    right_inv_ref,
+    twid_cos_ref,
+    twid_sin_ref,
+    features_ref,
+    value_out,
+    first_out,
+    second_out,
+    out_weight_out,
+    small_out,
+    recv,
+    outs,
+    small_part,
+    small_recv,
+    small_sum,
+    in_send,
+    in_recv,
+    out_send,
+    out_recv,
+    part_send,
+    part_recv,
+    sum_send,
+    sum_recv,
+):
+    n = devices
+    me = lax.axis_index("seq")
+    width = RADIX
+    seq_len = n * width
+    groups = channels // GROUP
+    rows_half = 2 * n * GROUP
+    half_rows = n * GROUP
+    bf16 = jnp.bfloat16
+    f32 = jnp.float32
+
+    barrier = pltpu.get_barrier_semaphore()
+
+    def greet(step, carry):
+        pl.semaphore_signal(
+            barrier, inc=1, device_id={"seq": lax.rem(me + step, n)}, device_id_type=MESH
+        )
+        return carry
+
+    lax.fori_loop(1, n, greet, 0)
+    pl.semaphore_wait(barrier, n - 1)
+
+    inputs = (value_ref, first_ref, cot_ref, second_ref)
+    outputs = (second_out, first_out, value_out)
+
+    def in_copy(at, peer, slot):
+        return pltpu.make_async_remote_copy(
+            src_ref=inputs[at].at[pl.ds(pl.multiple_of(peer * channels, channels), channels), :],
+            dst_ref=recv.at[at, slot],
+            send_sem=in_send.at[at, peer],
+            recv_sem=in_recv.at[at, slot],
+            device_id={"seq": peer},
+            device_id_type=MESH,
+        )
+
+    def out_copy(at, peer, slot):
+        return pltpu.make_async_remote_copy(
+            src_ref=outs.at[at, peer],
+            dst_ref=outputs[at].at[pl.ds(pl.multiple_of(slot * channels, channels), channels), :],
+            send_sem=out_send.at[at, peer],
+            recv_sem=out_recv.at[at, slot],
+            device_id={"seq": peer},
+            device_id_type=MESH,
+        )
+
+    def part_copy(peer, slot):
+        return pltpu.make_async_remote_copy(
+            src_ref=small_part.at[peer],
+            dst_ref=small_recv.at[slot],
+            send_sem=part_send.at[peer],
+            recv_sem=part_recv.at[slot],
+            device_id={"seq": peer},
+            device_id_type=MESH,
+        )
+
+    def sum_copy(peer, slot):
+        return pltpu.make_async_remote_copy(
+            src_ref=small_sum,
+            dst_ref=small_out.at[slot],
+            send_sem=sum_send.at[peer],
+            recv_sem=sum_recv.at[slot],
+            device_id={"seq": peer},
+            device_id_type=MESH,
+        )
+
+    def for_peers(action):
+        def body(step, carry):
+            action(lax.rem(me + step, n))
+            return carry
+
+        lax.fori_loop(1, n, body, 0)
+
+    for at in range(4):
+        for_peers(lambda peer, at=at: in_copy(at, peer, me).start())
+    own_rows = pl.ds(pl.multiple_of(me * channels, channels), channels)
+    for at in range(4):
+        recv[at, me] = inputs[at][own_rows, :]
+
+    features = features_ref[...]
+    pre_one = wide_dot(pos_weight_ref[...], features_ref[0:features_used, :]) + as_column(
+        pos_bias_ref[...], 64
+    )
+    act_one, slope_one = sin_cos(pre_one)
+    pre_two = wide_dot(mid_weight_ref[...], act_one) + as_column(mid_bias_ref[...], 64)
+    act_two, slope_two = sin_cos(pre_two)
+
+    first_row = me * (2 * channels)
+    own_weight = jnp.concatenate(
+        [out_weight_ref[pl.ds(first_row + o, channels, stride=2), :] for o in range(2)], axis=0
+    )
+    filter_rows = rates_ref.shape[1]
+    lane = lax.broadcasted_iota(jnp.int32, (2 * channels, filter_rows), 1)
+    row = lax.broadcasted_iota(jnp.int32, (2 * channels, filter_rows), 0)
+    wanted = jnp.where(row < channels, 2 * row, 2 * (row - channels) + 1) + first_row
+    own_rates = jnp.sum(jnp.where(lane == wanted, rates_ref[...], 0.0), axis=1, keepdims=True)
+    ramp = lax.broadcasted_iota(jnp.int32, (1, seq_len), 1).astype(f32) * (1.0 / seq_len)
+    window = jnp.exp(-own_rates * ramp)
+    filters = (wide_dot(own_weight, act_two) * window).astype(bf16)
+
+    def to_sections(rows):
+        return jnp.concatenate(
+            [
+                jnp.concatenate(
+                    [
+                        rows[GROUP * g : GROUP * (g + 1), width * at : width * (at + 1)]
+                        for at in range(n)
+                    ],
+                    axis=0,
+                )
+                for g in range(groups)
+            ],
+            axis=1,
+        )
+
+    def from_sections(data):
+        return jnp.concatenate(
+            [
+                jnp.concatenate(
+                    [
+                        data[GROUP * at : GROUP * (at + 1), width * g : width * (g + 1)]
+                        for at in range(n)
+                    ],
+                    axis=1,
+                )
+                for g in range(groups)
+            ],
+            axis=0,
+        )
+
+    def forward(data):
+        stage = short_dot(left_fwd_ref[...], data)
+        cos, sin = twid_cos_ref[...], twid_sin_ref[...]
+        result = []
+        for g in range(groups):
+            real = stage[:rows_half, width * g : width * (g + 1)]
+            imag = stage[rows_half:, width * g : width * (g + 1)]
+            real_b = (real * cos + imag * sin).astype(bf16)
+            imag_b = (imag * cos - real * sin).astype(bf16)
+            spectrum = short_dot(jnp.concatenate([real_b, imag_b], axis=1), right_fwd_ref[...])
+            result.append((spectrum[:, :width], spectrum[:, width:]))
+        return result
+
+    def inverse(left, right, conj_left, conj_right):
+        cos, sin = twid_cos_ref[...], twid_sin_ref[...]
+        sections = []
+        for g in range(groups):
+            real_p, imag_p = spectral_product(left[g], right[g], conj_left, conj_right)
+            stage = short_dot(jnp.concatenate([real_p, imag_p], axis=1), right_inv_ref[...])
+            real, imag = stage[:, :width], stage[:, width:]
+            real_r = (real * cos - imag * sin).astype(bf16)
+            imag_r = (imag * cos + real * sin).astype(bf16)
+            sections.append(jnp.concatenate([real_r, imag_r], axis=0))
+        return short_dot(left_inv_ref[...], jnp.concatenate(sections, axis=1))
+
+    def arrived(at):
+        for_peers(lambda peer: in_copy(at, peer, peer).wait_recv())
+        return jnp.concatenate(
+            [
+                recv[at, :, GROUP * g : GROUP * (g + 1), :].reshape(half_rows, width)
+                for g in range(groups)
+            ],
+            axis=1,
+        )
+
+    def send_out(at, data):
+        for g in range(groups):
+            outs[at, :, GROUP * g : GROUP * (g + 1), :] = data[
+                :, width * g : width * (g + 1)
+            ].reshape(n, GROUP, width)
+        for_peers(lambda peer: out_copy(at, peer, me).start())
+        outputs[at][own_rows, :] = outs[at, me]
+
+    spec_one = forward(to_sections(filters[:channels]))
+    spec_two = forward(to_sections(filters[channels:]))
+    spec_val = forward(arrived(0))
+    conv_one = inverse(spec_one, spec_val, False, False)
+    first = arrived(1).astype(f32)
+    spec_gated = forward((first * conv_one).astype(bf16))
+    conv_two = inverse(spec_two, spec_gated, False, False)
+    cot = arrived(2).astype(f32)
+    send_out(0, (cot * conv_two).astype(bf16))
+    second = arrived(3).astype(f32)
+    spec_gtwo = forward((cot * second).astype(bf16))
+    gated_grad = inverse(spec_two, spec_gtwo, True, False)
+    send_out(1, (gated_grad * conv_one).astype(bf16))
+    spec_gone = forward((gated_grad * first).astype(bf16))
+    send_out(2, inverse(spec_one, spec_gone, True, False).astype(bf16))
+    filt_one = from_sections(inverse(spec_gone, spec_val, False, True))
+    filt_two = from_sections(inverse(spec_gtwo, spec_gated, False, True))
+    filter_grad = jnp.concatenate([filt_one, filt_two], axis=0) * window * (1.0 / seq_len)
+
+    pre_two_grad = contract_dims(own_weight, filter_grad, 0, 0) * slope_two
+    pre_one_grad = contract_dims(mid_weight_ref[...], pre_two_grad, 0, 0) * slope_one
+    ones_row = jnp.where(
+        lax.broadcasted_iota(jnp.int32, (64, seq_len), 0) == features_used + 1, 1.0, 0.0
+    )
+    small = contract_dims(pre_two_grad, jnp.concatenate([act_one, ones_row], axis=0), 1, 1)
+    small = small + contract_dims(
+        pre_one_grad, jnp.concatenate([jnp.zeros_like(features), features], axis=0), 1, 1
+    )
+    share = small.shape[0] // n
+    for at in range(n):
+        small_part[at] = small[share * at : share * (at + 1), :]
+    for_peers(lambda peer: part_copy(peer, me).start())
+    small_recv[me] = small_part[me]
+
+    weight_grad = contract_dims(filter_grad, act_two, 1, 1)
+    for o in range(2):
+        out_weight_out[pl.ds(o, channels, stride=2), :] = weight_grad[
+            channels * o : channels * (o + 1)
+        ]
+
+    for_peers(lambda peer: part_copy(peer, peer).wait_recv())
+    total = small_recv[0]
+    for at in range(1, n):
+        total = total + small_recv[at]
+    small_sum[...] = total
+    small_out[me] = total
+    for_peers(lambda peer: sum_copy(peer, me).start())
+
+    for at in range(4):
+        for_peers(lambda peer, at=at: in_copy(at, peer, me).wait_send())
+    for at in range(3):
+        for_peers(lambda peer, at=at: out_copy(at, peer, me).wait_send())
+        for_peers(lambda peer, at=at: out_copy(at, peer, peer).wait_recv())
+    for_peers(lambda peer: part_copy(peer, me).wait_send())
+    for_peers(lambda peer: sum_copy(peer, me).wait_send())
+    for_peers(lambda peer: sum_copy(peer, peer).wait_recv())
+
+
+def on_device(
+    value_branch,
+    first_gate,
+    second_gate,
+    out_cotangent,
+    pos_weight,
+    pos_bias,
+    mid_weight,
+    mid_bias,
+    out_weight,
+    decay_rates,
+):
+    model_width, tok_dev = value_branch.shape
+    devices = lax.axis_size("seq")
+    channels = model_width // devices
+    hidden, features_used = pos_weight.shape
+    fits = (
+        tok_dev == RADIX
+        and devices == 16
+        and channels == 2 * GROUP
+        and hidden == 64
+        and features_used <= 62
+        and out_weight.shape == (2 * model_width, 64)
+    )
+    if not fits:
+        return on_device_plain(
+            value_branch,
+            first_gate,
+            second_gate,
+            out_cotangent,
+            pos_weight,
+            pos_bias,
+            mid_weight,
+            mid_bias,
+            out_weight,
+            decay_rates,
+        )
+    seq_len = tok_dev * devices
+    freq_rows = 2 * devices
+    tables = numpy_tables(freq_rows, RADIX, seq_len, (features_used - 1) // 2, GROUP)
+    share = hidden // devices
+    dma = pltpu.SemaphoreType.DMA
+    vmem = pl.BlockSpec(memory_space=pltpu.VMEM)
+    value_out, first_out, second_out, weight_out, small = pl.pallas_call(
+        functools.partial(operator_kernel, devices, channels, features_used),
+        out_shape=[jax.ShapeDtypeStruct((model_width, tok_dev), jnp.bfloat16)] * 3
+        + [
+            jax.ShapeDtypeStruct((2 * channels, hidden), jnp.float32),
+            jax.ShapeDtypeStruct((devices, share, 2 * hidden), jnp.float32),
+        ],
+        in_specs=[vmem] * 17,
+        out_specs=[vmem] * 5,
+        scratch_shapes=[
+            pltpu.VMEM((4, devices, channels, RADIX), jnp.bfloat16),
+            pltpu.VMEM((3, devices, channels, RADIX), jnp.bfloat16),
+            pltpu.VMEM((devices, share, 2 * hidden), jnp.float32),
+            pltpu.VMEM((devices, share, 2 * hidden), jnp.float32),
+            pltpu.VMEM((share, 2 * hidden), jnp.float32),
+            dma((4, devices)),
+            dma((4, devices)),
+            dma((3, devices)),
+            dma((3, devices)),
+            dma((devices,)),
+            dma((devices,)),
+            dma((devices,)),
+            dma((devices,)),
+        ],
+        compiler_params=pltpu.CompilerParams(
+            collective_id=0, has_side_effects=True, vmem_limit_bytes=50 * 1024 * 1024
+        ),
+    )(
+        value_branch,
+        first_gate,
+        second_gate,
+        out_cotangent,
+        pos_weight,
+        pos_bias.reshape(1, hidden),
+        mid_weight,
+        mid_bias.reshape(1, hidden),
+        out_weight,
+        decay_rates.reshape(1, 2 * model_width),
+        *[jnp.asarray(table) for table in tables],
+    )
+    small = small.reshape(hidden, 2 * hidden)
+    at = hidden + features_used
+    return (
+        value_out,
+        first_out,
+        second_out,
+        small[:, hidden:at],
+        small[:, at],
+        small[:, :hidden],
+        small[:, at + 1],
+        weight_out,
+    )
+
+
 def solution(mesh):
     in_specs = (
         P(None, ("dp", "seq")),

time: 215 us -> 56 us (0.26)
  blocking collectives: 74.4 us -> 0 us
  waiting for transfers between devices: 52.5 us -> 0 us
  starting transfers between devices: 40.3 us -> 0 us
  Pallas kernels: 0 us -> 39.7 us
  matrix products: 17.9 us -> 0 us
  between operations: 14.5 us -> 0.76 us
  local copies, waits for them, and re-layouts: 7.72 us -> 15.2 us
  other arithmetic: 5.94 us -> 0 us
    psum x1 -> x0, blocking collectives: 74.4 us -> none  [on_device(): lax.psum((partials[0], partials[1], partials[2], partials[3]), 'seq')]
    all_to_all x9 -> x0, waiting for transfers between devices: 52.5 us -> none  [the longest x1 8.42 us: on_device(): lax.all_to_all(filter_grad_ch.astype(jnp.bfloat16), 'seq', split_axis=1,...]
    all_to_all x9 -> x0, starting transfers between devices: 40.3 us -> none  [the longest x1 8.46 us: on_device(): lax.all_to_all(out_cotangent, 'seq', split_axis=0, concat_axis=1, tiled=T...]
    pallas_call x0 -> x1, Pallas kernels: none -> 39.7 us  [on_device(): pl.pallas_call(functools.partial(operator_kernel, devices, channels, feat...]
    dot_general x30 -> x0, matrix products: 17.9 us -> none  [the longest x5 4.84 us: forward_spectrum(): jnp.einsum('kn,rnm->rkm', left_table, shaped, preferred_element_type=jnp....]
    unnamed x41 -> x38, local copies, waits for them, and re-layouts: 3.41 us -> 14.4 us
    convert_element_type x5 -> x0, local copies, waits for them, and re-layouts: 3.7 us -> none  [the longest x1 0.86 us: on_device(): local_filters = (jnp.dot(out_weight, act_two, precision=lax.Precision.HIG...]
    convert_element_type x14 -> x0, other arithmetic: 3.37 us -> none  [the longest x4 1.1 us: spectral_product(): return (real_part.astype(jnp.bfloat16), imag_part.astype(jnp.bfloat16))]
  transfers between devices with their start and end apart: 10 -> 0, of which waited for: 9 -> 0; matrix products, arithmetic and copies ran while one was open for 9% -> 0% of each run, Pallas kernels for 0% -> 0%
where the time goes in v1:
time: 56 us; the launch traced here: 55.6 us
  Pallas kernels  39.7 us (71%)
  local copies, waits for them, and re-layouts  15.2 us (27%)
  between operations  0.76 us (1%)
    pallas_call x1, Pallas kernels, on_device(): pl.pallas_call(functools.partial(operator_kernel, devices, channels, feat...  39.7 us
    unnamed x38, local copies, waits for them, and re-layouts  14.4 us

profile of v1, /device:TPU:0, one launch (start us, length us, event | category | flops | bytes accessed | tf_op | source)
XLA Modules:
  0.0 55.6 jit_solution(12474113264318771355)
XLA Ops:
  0.6 0.0 copy-start
  0.6 0.9 %copy.28.pos_weight_ref = f32[64,33]{1,0:T(8,128)S(1)} copy(f32[64,33]{0,1:T(8,128)} %param.21) | data formatting | bytes 16896 | tf_op args[4]
  1.5 0.0 copy-start.11
  1.5 0.0 copy-start.13
  1.6 1.2 %copy.29.out_weight_ref = f32[1024,64]{1,0:T(8,128)S(1)} copy(f32[1024,64]{0,1:T(8,128)} %param.25) | data formatting | bytes 524288 | tf_op args[8]
  2.8 0.0 copy-start.1
  2.8 1.0 %copy-done.1 = bf16[256,1024]{1,0:T(8,128)(2,1)S(1)} copy-done((bf16[256,1024]{1,0:T(8,128)(2,1)S(1)}, bf16[256,1024]{1,0:T(8,128)(2,1)}, u32[]{:S(2)}) %copy-start.1) | copy-done | bytes 524312
  3.9 1.0 %copy-done.2 = bf16[1024,256]{1,0:T(8,128)(2,1)S(1)} copy-done((bf16[1024,256]{1,0:T(8,128)(2,1)S(1)}, bf16[1024,256]{1,0:T(8,128)(2,1)}, u32[]{:S(2)}) %copy-start.2) | copy-done | bytes 524312
  4.9 0.9 %copy-done.4 = f32[512,128]{1,0:T(8,128)S(1)} copy-done((f32[512,128]{1,0:T(8,128)S(1)}, f32[512,128]{1,0:T(8,128)}, u32[]{:S(2)}) %copy-start.4) | copy-done | bytes 262168
  5.9 0.9 %copy-done.5 = bf16[512,128]{1,0:T(8,128)(2,1)S(1)} copy-done((bf16[512,128]{1,0:T(8,128)(2,1)S(1)}, bf16[512,128]{1,0:T(8,128)(2,1)}, u32[]{:S(2)}) %copy-start.5) | copy-done | bytes 131096
  6.8 0.9 %copy-done.6 = bf16[512,128]{1,0:T(8,128)(2,1)S(1)} copy-done((bf16[512,128]{1,0:T(8,128)(2,1)S(1)}, bf16[512,128]{1,0:T(8,128)(2,1)}, u32[]{:S(2)}) %copy-start.6) | copy-done | bytes 131096
  7.7 0.9 %copy-done.7 = bf16[512,128]{1,0:T(8,128)(2,1)S(1)} copy-done((bf16[512,128]{1,0:T(8,128)(2,1)S(1)}, bf16[512,128]{1,0:T(8,128)(2,1)}, u32[]{:S(2)}) %copy-start.7) | copy-done | bytes 131096
  8.6 0.9 %copy-done.8 = bf16[512,128]{1,0:T(8,128)(2,1)S(1)} copy-done((bf16[512,128]{1,0:T(8,128)(2,1)S(1)}, bf16[512,128]{1,0:T(8,128)(2,1)}, u32[]{:S(2)}) %copy-start.8) | copy-done | bytes 131096
  9.5 0.9 %copy-done.9 = bf16[256,256]{1,0:T(8,128)(2,1)S(1)} copy-done((bf16[256,256]{1,0:T(8,128)(2,1)S(1)}, bf16[256,256]{1,0:T(8,128)(2,1)}, u32[]{:S(2)}) %copy-start.9) | copy-done | bytes 131096
  10.4 0.9 %copy-done.10 = bf16[256,256]{1,0:T(8,128)(2,1)S(1)} copy-done((bf16[256,256]{1,0:T(8,128)(2,1)S(1)}, bf16[256,256]{1,0:T(8,128)(2,1)}, u32[]{:S(2)}) %copy-start.10) | copy-done | bytes 131096
  11.3 39.7 %shard_map.224 = (bf16[512,128]{1,0:T(8,128)(2,1)S(1)}, bf16[512,128]{1,0:T(8,128)(2,1)S(1)}, bf16[512,128]{1,0:T(8,128)(2,1)S(1)}, f32[64,64]{1,0:T(8,128)S(1)}, f32[16,4,128]{2,1,0:T(4,128)S(1)}) custom-call(bf16[512,128]{1,0:T(8,128)(2,1)S(1)} %copy-done.5, bf16[512,128]{1,0:T(8,128)(2,1)S(1)} %copy-done.6, bf16[512,128]{1,0:T(8,128)(2,1)S(1)} %copy-done.7, ...), custom_call_target="tpu_custom_call" | custom-call | tf_op jit(solution)/shard_map/pallas_call | solution.py:610
  51.0 0.7 %slice_reduce_fusion = (f32[64]{0:T(128)}, f32[64]{0:T(128)}) fusion(f32[64,128]{1,0:T(8,128)S(1)} %bitcast.5), kind=kLoop, calls=%fused_computation | loop fusion | bytes 1024 | tf_op jit(solution)/shard_map/slice | solution.py:659
  51.7 0.1 slice.16
  51.8 0.7 %copy.30 = f32[64,33]{0,1:T(8,128)} copy(f32[64,33]{1,0:T(8,128)S(1)} %slice.16) | data formatting | bytes 16896
  52.4 0.7 %copy.36 = bf16[512,128]{1,0:T(8,128)(2,1)} copy(bf16[512,128]{1,0:T(8,128)(2,1)S(1)} %get-tuple-element.44) | data formatting | bytes 262144
  53.1 0.7 %copy.37 = bf16[512,128]{1,0:T(8,128)(2,1)} copy(bf16[512,128]{1,0:T(8,128)(2,1)S(1)} %get-tuple-element.45) | data formatting | bytes 262144
  53.8 0.7 %copy.38 = bf16[512,128]{1,0:T(8,128)(2,1)} copy(bf16[512,128]{1,0:T(8,128)(2,1)S(1)} %get-tuple-element.46) | data formatting | bytes 262144
  54.4 0.6 %copy.39 = f32[64,64]{1,0:T(8,128)} copy(f32[64,64]{1,0:T(8,128)S(1)} %bitcast.7) | data formatting | bytes 32768
  55.0 0.6 %copy.40 = f32[64,64]{1,0:T(8,128)} copy(f32[64,64]{1,0:T(8,128)S(1)} %get-tuple-element.51) | data formatting | bytes 32768
  (17 shorter events, 0.0 us)
Async XLA Ops:
  0.6 2.1 %copy-start = (f32[64,2048]{1,0:T(8,128)S(1)}, f32[64,2048]{1,0:T(8,128)}, u32[]{:S(2)}) copy-start(f32[64,2048]{1,0:T(8,128)} %constant.20.clone.features_ref) | copy-start | bytes 1572868
  1.5 1.3 %copy-start.3 = (f32[512,128]{1,0:T(8,128)S(1)}, f32[512,128]{1,0:T(8,128)}, u32[]{:S(2)}) copy-start(f32[512,128]{1,0:T(8,128)} %constant.19.clone.twid_sin_ref) | copy-start | bytes 786436
  1.5 1.3 %copy-start.11 = (f32[64,64]{1,0:T(8,128)S(1)}, f32[64,64]{1,0:T(8,128)}, u32[]{:S(2)}) copy-start(f32[64,64]{1,0:T(8,128)} %mid_weight_ref.1) | copy-start | bytes 49156
  1.5 1.3 %copy-start.12 = (f32[1024]{0:T(1024)S(1)}, f32[1024]{0:T(1024)}, u32[]{:S(2)}) copy-start(f32[1024]{0:T(1024)} %param.26) | copy-start | bytes 12292
  1.5 1.3 %copy-start.13 = (f32[64]{0:T(128)S(1)}, f32[64]{0:T(128)}, u32[]{:S(2)}) copy-start(f32[64]{0:T(128)} %param.22) | copy-start | bytes 772
  1.6 1.3 %copy-start.14 = (f32[64]{0:T(128)S(1)}, f32[64]{0:T(128)}, u32[]{:S(2)}) copy-start(f32[64]{0:T(128)} %param.24) | copy-start | bytes 772
  2.8 1.0 %copy-start.1 = (bf16[256,1024]{1,0:T(8,128)(2,1)S(1)}, bf16[256,1024]{1,0:T(8,128)(2,1)}, u32[]{:S(2)}) copy-start(bf16[256,1024]{1,0:T(8,128)(2,1)} %constant.15.clone.left_inv_ref) | copy-start | bytes 1572868
  3.9 1.0 %copy-start.2 = (bf16[1024,256]{1,0:T(8,128)(2,1)S(1)}, bf16[1024,256]{1,0:T(8,128)(2,1)}, u32[]{:S(2)}) copy-start(bf16[1024,256]{1,0:T(8,128)(2,1)} %constant.14.clone.left_fwd_ref) | copy-start | bytes 1572868
  4.9 0.9 %copy-start.4 = (f32[512,128]{1,0:T(8,128)S(1)}, f32[512,128]{1,0:T(8,128)}, u32[]{:S(2)}) copy-start(f32[512,128]{1,0:T(8,128)} %constant.18.clone.twid_cos_ref) | copy-start | bytes 786436
  5.8 0.9 %copy-start.5 = (bf16[512,128]{1,0:T(8,128)(2,1)S(1)}, bf16[512,128]{1,0:T(8,128)(2,1)}, u32[]{:S(2)}) copy-start(bf16[512,128]{1,0:T(8,128)(2,1)} %value_ref.1) | copy-start | bytes 393220
  6.8 0.9 %copy-start.6 = (bf16[512,128]{1,0:T(8,128)(2,1)S(1)}, bf16[512,128]{1,0:T(8,128)(2,1)}, u32[]{:S(2)}) copy-start(bf16[512,128]{1,0:T(8,128)(2,1)} %first_ref.1) | copy-start | bytes 393220
  7.7 0.9 %copy-start.7 = (bf16[512,128]{1,0:T(8,128)(2,1)S(1)}, bf16[512,128]{1,0:T(8,128)(2,1)}, u32[]{:S(2)}) copy-start(bf16[512,128]{1,0:T(8,128)(2,1)} %second_ref.1) | copy-start | bytes 393220
  8.6 0.9 %copy-start.8 = (bf16[512,128]{1,0:T(8,128)(2,1)S(1)}, bf16[512,128]{1,0:T(8,128)(2,1)}, u32[]{:S(2)}) copy-start(bf16[512,128]{1,0:T(8,128)(2,1)} %cot_ref.1) | copy-start | bytes 393220
  9.5 0.9 %copy-start.9 = (bf16[256,256]{1,0:T(8,128)(2,1)S(1)}, bf16[256,256]{1,0:T(8,128)(2,1)}, u32[]{:S(2)}) copy-start(bf16[256,256]{1,0:T(8,128)(2,1)} %constant.17.clone.right_inv_ref) | copy-start | bytes 393220
  10.4 0.9 %copy-start.10 = (bf16[256,256]{1,0:T(8,128)(2,1)S(1)}, bf16[256,256]{1,0:T(8,128)(2,1)}, u32[]{:S(2)}) copy-start(bf16[256,256]{1,0:T(8,128)(2,1)} %constant.16.clone.right_fwd_ref) | copy-start | bytes 393220

commit v2 on v1

--- a/solution.py
+++ b/solution.py
@@ -13,7 +13,6 @@
 RADIX = 128
 GROUP = 16
 MESH = pl.DeviceIdType.MESH
-HIGHEST = lax.Precision.HIGHEST
 
 
 def make_tables(freq_rows, radix):
@@ -243,14 +242,17 @@
     positions = np.arange(seq_len)
     band = np.arange(1, bands + 1)
     angles = (band[:, None] * positions[None, :] % seq_len) * (2.0 * np.pi / seq_len)
-    features = np.zeros((64, seq_len))
+    features = np.zeros((64, seq_len), np.float32)
     features[0] = positions / seq_len
     features[1 : bands + 1] = np.cos(angles)
     features[bands + 1 : 2 * bands + 1] = np.sin(angles)
-    features[2 * bands + 1] = 1.0
+    features[2 * bands + 1 : 2 * bands + 3] = 1.0
+    upper = features.astype(ml_dtypes.bfloat16)
+    lower = (features - upper.astype(np.float32)).astype(ml_dtypes.bfloat16)
+    features = np.concatenate([upper, lower], axis=0)
     low = [table.astype(ml_dtypes.bfloat16) for table in (left_fwd, left_inv, right_fwd, right_inv)]
-    wide = [table.astype(np.float32) for table in (twid_cos, twid_sin, features)]
-    return low + wide
+    wide = [table.astype(np.float32) for table in (twid_cos, twid_sin)]
+    return low + wide + [features]
 
 
 def sin_cos(x):
@@ -269,21 +271,27 @@
     return sign * rest * odd, sign * even
 
 
-def wide_dot(left, right):
-    return jnp.dot(left, right, precision=HIGHEST, preferred_element_type=jnp.float32)
-
-
 def short_dot(left, right):
     return jnp.dot(left, right, preferred_element_type=jnp.float32)
 
 
 def contract_dims(left, right, left_dim, right_dim):
     return lax.dot_general(
-        left,
-        right,
-        (((left_dim,), (right_dim,)), ((), ())),
-        precision=HIGHEST,
-        preferred_element_type=jnp.float32,
+        left, right, (((left_dim,), (right_dim,)), ((), ())), preferred_element_type=jnp.float32
+    )
+
+
+def halves(x):
+    upper = x.astype(jnp.bfloat16)
+    return upper, (x - upper.astype(jnp.float32)).astype(jnp.bfloat16)
+
+
+def split_dot(left, right):
+    return contract_dims(
+        jnp.concatenate([left[0], left[1], left[0]], axis=0),
+        jnp.concatenate([right[0], right[0], right[1]], axis=0),
+        0,
+        0,
     )
 
 
@@ -303,19 +311,19 @@
     first_ref,
     second_ref,
     cot_ref,
-    pos_weight_ref,
-    pos_bias_ref,
-    mid_weight_ref,
-    mid_bias_ref,
-    out_weight_ref,
-    rates_ref,
-    left_fwd_ref,
-    left_inv_ref,
-    right_fwd_ref,
-    right_inv_ref,
-    twid_cos_ref,
-    twid_sin_ref,
-    features_ref,
+    pos_weight_hbm,
+    pos_bias_hbm,
+    mid_weight_hbm,
+    mid_bias_hbm,
+    out_weight_hbm,
+    rates_hbm,
+    left_fwd_hbm,
+    left_inv_hbm,
+    right_fwd_hbm,
+    right_inv_hbm,
+    twid_cos_hbm,
+    twid_sin_hbm,
+    features_hbm,
     value_out,
     first_out,
     second_out,
@@ -334,6 +342,22 @@
     part_recv,
     sum_send,
     sum_recv,
+    pos_weight_ref,
+    pos_bias_ref,
+    mid_weight_ref,
+    mid_bias_ref,
+    out_weight_ref,
+    rates_ref,
+    left_fwd_ref,
+    left_inv_ref,
+    right_fwd_ref,
+    right_inv_ref,
+    twid_cos_ref,
+    twid_sin_ref,
+    features_ref,
+    pos_table,
+    load_sem,
+    own_sem,
 ):
     n = devices
     me = lax.axis_index("seq")
@@ -354,9 +378,41 @@
         return carry
 
     lax.fori_loop(1, n, greet, 0)
+
+    inputs = (value_ref, first_ref, cot_ref, second_ref)
+    own_rows = pl.ds(pl.multiple_of(me * channels, channels), channels)
+    pair = lax.rem(me, 2)
+    column = me // 2
+    loads = [
+        pltpu.make_async_copy(source, target, load_sem.at[at])
+        for at, (source, target) in enumerate(
+            (
+                (pos_weight_hbm, pos_weight_ref),
+                (pos_bias_hbm, pos_bias_ref),
+                (features_hbm, features_ref),
+                (mid_weight_hbm, mid_weight_ref),
+                (mid_bias_hbm, mid_bias_ref),
+                (out_weight_hbm.at[:, pl.ds(pl.multiple_of(column * 128, 128), 128)], out_weight_ref),
+                (rates_hbm, rates_ref),
+                (left_fwd_hbm, left_fwd_ref),
+                (right_fwd_hbm, right_fwd_ref),
+                (twid_cos_hbm, twid_cos_ref),
+                (twid_sin_hbm, twid_sin_ref),
+                (right_inv_hbm, right_inv_ref),
+                (left_inv_hbm, left_inv_ref),
+            )
+        )
+    ]
+    for load in loads:
+        load.start()
+    own_loads = [
+        pltpu.make_async_copy(inputs[at].at[own_rows, :], recv.at[at, me], own_sem.at[at])
+        for at in range(4)
+    ]
+    for load in own_loads:
+        load.start()
     pl.semaphore_wait(barrier, n - 1)
 
-    inputs = (value_ref, first_ref, cot_ref, second_ref)
     outputs = (second_out, first_out, value_out)
 
     def in_copy(at, peer, slot):
@@ -408,30 +464,40 @@
 
     for at in range(4):
         for_peers(lambda peer, at=at: in_copy(at, peer, me).start())
-    own_rows = pl.ds(pl.multiple_of(me * channels, channels), channels)
-    for at in range(4):
-        recv[at, me] = inputs[at][own_rows, :]
-
-    features = features_ref[...]
-    pre_one = wide_dot(pos_weight_ref[...], features_ref[0:features_used, :]) + as_column(
-        pos_bias_ref[...], 64
-    )
+
+    pos_table[...] = jnp.zeros_like(pos_table)
+    for load in loads[:7]:
+        load.wait()
+    pos_table[0:features_used, :] = pos_weight_ref[...]
+    pos_table[features_used : features_used + 1, :] = pos_bias_ref[...]
+    features = features_ref[0:64, :]
+    pre_one = split_dot(halves(pos_table[...]), (features, features_ref[64:128, :]))
     act_one, slope_one = sin_cos(pre_one)
-    pre_two = wide_dot(mid_weight_ref[...], act_one) + as_column(mid_bias_ref[...], 64)
+    act_one = halves(act_one)
+    mid_weight = mid_weight_ref[...]
+    pre_two = split_dot(halves(mid_weight.T), act_one) + as_column(mid_bias_ref[...], 64)
     act_two, slope_two = sin_cos(pre_two)
-
-    first_row = me * (2 * channels)
-    own_weight = jnp.concatenate(
-        [out_weight_ref[pl.ds(first_row + o, channels, stride=2), :] for o in range(2)], axis=0
-    )
-    filter_rows = rates_ref.shape[1]
-    lane = lax.broadcasted_iota(jnp.int32, (2 * channels, filter_rows), 1)
-    row = lax.broadcasted_iota(jnp.int32, (2 * channels, filter_rows), 0)
-    wanted = jnp.where(row < channels, 2 * row, 2 * (row - channels) + 1) + first_row
-    own_rates = jnp.sum(jnp.where(lane == wanted, rates_ref[...], 0.0), axis=1, keepdims=True)
+    act_two = halves(act_two)
+
+    def wanted(row):
+        return jnp.where(row < channels, 2 * row, 2 * (row - channels) + 1) + 2 * channels * pair
+
+    lane = lax.broadcasted_iota(jnp.int32, (2 * channels, 128), 1)
+    row = lax.broadcasted_iota(jnp.int32, (2 * channels, 128), 0)
+    rates_row = rates_ref[pl.ds(column, 1), :]
+    own_rates = jnp.sum(jnp.where(lane == wanted(row), rates_row, 0.0), axis=1, keepdims=True)
+    pick = lax.broadcasted_iota(jnp.int32, (128, 2 * channels), 0) == wanted(
+        lax.broadcasted_iota(jnp.int32, (128, 2 * channels), 1)
+    )
+    pick = jnp.where(pick, 1.0, 0.0).astype(bf16)
+    own_weight = tuple(
+        short_dot(half, pick).astype(bf16) for half in halves(out_weight_ref[...])
+    )
     ramp = lax.broadcasted_iota(jnp.int32, (1, seq_len), 1).astype(f32) * (1.0 / seq_len)
     window = jnp.exp(-own_rates * ramp)
-    filters = (wide_dot(own_weight, act_two) * window).astype(bf16)
+    filters = (split_dot(own_weight, act_two) * window).astype(bf16)
+    for load in loads[7:]:
+        load.wait()
 
     def to_sections(rows):
         return jnp.concatenate(
@@ -489,6 +555,7 @@
         return short_dot(left_inv_ref[...], jnp.concatenate(sections, axis=1))
 
     def arrived(at):
+        own_loads[at].wait()
         for_peers(lambda peer: in_copy(at, peer, peer).wait_recv())
         return jnp.concatenate(
             [
@@ -525,22 +592,25 @@
     filt_two = from_sections(inverse(spec_gtwo, spec_gated, False, True))
     filter_grad = jnp.concatenate([filt_one, filt_two], axis=0) * window * (1.0 / seq_len)
 
-    pre_two_grad = contract_dims(own_weight, filter_grad, 0, 0) * slope_two
-    pre_one_grad = contract_dims(mid_weight_ref[...], pre_two_grad, 0, 0) * slope_one
-    ones_row = jnp.where(
-        lax.broadcasted_iota(jnp.int32, (64, seq_len), 0) == features_used + 1, 1.0, 0.0
-    )
-    small = contract_dims(pre_two_grad, jnp.concatenate([act_one, ones_row], axis=0), 1, 1)
-    small = small + contract_dims(
-        pre_one_grad, jnp.concatenate([jnp.zeros_like(features), features], axis=0), 1, 1
-    )
+    filter_grad = filter_grad.astype(bf16)
+    pre_two_grad = (short_dot(own_weight[0], filter_grad) * slope_two).astype(bf16)
+    pre_one_grad = contract_dims(mid_weight.astype(bf16), pre_two_grad, 0, 0) * slope_one
+    both = contract_dims(
+        jnp.concatenate([pre_two_grad, pre_one_grad.astype(bf16)], axis=0),
+        jnp.concatenate([act_one[0], features], axis=0),
+        1,
+        1,
+    )
+    lane = lax.broadcasted_iota(jnp.int32, (64, 128), 1)
+    from_two = (lane < 64) | (lane == 64 + features_used + 1)
+    small = jnp.where(from_two, both[:64], both[64:])
     share = small.shape[0] // n
     for at in range(n):
         small_part[at] = small[share * at : share * (at + 1), :]
     for_peers(lambda peer: part_copy(peer, me).start())
     small_recv[me] = small_part[me]
 
-    weight_grad = contract_dims(filter_grad, act_two, 1, 1)
+    weight_grad = contract_dims(filter_grad, act_two[0], 1, 1)
     for o in range(2):
         out_weight_out[pl.ds(o, channels, stride=2), :] = weight_grad[
             channels * o : channels * (o + 1)
@@ -562,6 +632,47 @@
     for_peers(lambda peer: part_copy(peer, me).wait_send())
     for_peers(lambda peer: sum_copy(peer, me).wait_send())
     for_peers(lambda peer: sum_copy(peer, peer).wait_recv())
+
+
+def finish_kernel(
+    features_used,
+    value_in,
+    first_in,
+    second_in,
+    weight_in,
+    small_ref,
+    value_out,
+    first_out,
+    second_out,
+    weight_out,
+    pos_weight_out,
+    pos_bias_out,
+    mid_weight_out,
+    mid_bias_out,
+    sem,
+):
+    copies = [
+        pltpu.make_async_copy(source, target, sem.at[at])
+        for at, (source, target) in enumerate(
+            (
+                (value_in, value_out),
+                (first_in, first_out),
+                (second_in, second_out),
+                (weight_in, weight_out),
+            )
+        )
+    ]
+    for copy in copies:
+        copy.start()
+    small = small_ref[...]
+    turned = small.T
+    last = 64 + features_used
+    pos_weight_out[...] = turned[64:last]
+    pos_bias_out[...] = turned[last : last + 1]
+    mid_bias_out[...] = turned[last + 1 : last + 2]
+    mid_weight_out[...] = small[:, :64]
+    for copy in copies:
+        copy.wait()
 
 
 def on_device(
@@ -585,7 +696,7 @@
         and devices == 16
         and channels == 2 * GROUP
         and hidden == 64
-        and features_used <= 62
+        and features_used <= 61
         and out_weight.shape == (2 * model_width, 64)
     )
     if not fits:
@@ -607,6 +718,9 @@
     share = hidden // devices
     dma = pltpu.SemaphoreType.DMA
     vmem = pl.BlockSpec(memory_space=pltpu.VMEM)
+    hbm = pl.BlockSpec(memory_space=pltpu.HBM)
+    anywhere = pl.BlockSpec(memory_space=pl.ANY)
+    bf16, f32 = jnp.bfloat16, jnp.float32
     value_out, first_out, second_out, weight_out, small = pl.pallas_call(
         functools.partial(operator_kernel, devices, channels, features_used),
         out_shape=[jax.ShapeDtypeStruct((model_width, tok_dev), jnp.bfloat16)] * 3
@@ -614,7 +728,7 @@
             jax.ShapeDtypeStruct((2 * channels, hidden), jnp.float32),
             jax.ShapeDtypeStruct((devices, share, 2 * hidden), jnp.float32),
         ],
-        in_specs=[vmem] * 17,
+        in_specs=[hbm] * 17,
         out_specs=[vmem] * 5,
         scratch_shapes=[
             pltpu.VMEM((4, devices, channels, RADIX), jnp.bfloat16),
@@ -630,6 +744,16 @@
             dma((devices,)),
             dma((devices,)),
             dma((devices,)),
+            pltpu.VMEM((features_used, hidden), f32),
+            pltpu.VMEM((1, hidden), f32),
+            pltpu.VMEM((hidden, hidden), f32),
+            pltpu.VMEM((1, hidden), f32),
+            pltpu.VMEM((hidden, 128), f32),
+            pltpu.VMEM((2 * model_width // 128, 128), f32),
+            *[pltpu.VMEM(table.shape, table.dtype) for table in tables],
+            pltpu.VMEM((hidden, hidden), f32),
+            dma((13,)),
+            dma((4,)),
         ],
         compiler_params=pltpu.CompilerParams(
             collective_id=0, has_side_effects=True, vmem_limit_bytes=50 * 1024 * 1024
@@ -639,25 +763,39 @@
         first_gate,
         second_gate,
         out_cotangent,
-        pos_weight,
+        pos_weight.T,
         pos_bias.reshape(1, hidden),
         mid_weight,
         mid_bias.reshape(1, hidden),
-        out_weight,
-        decay_rates.reshape(1, 2 * model_width),
+        out_weight.T,
+        decay_rates.reshape(2 * model_width // 128, 128),
         *[jnp.asarray(table) for table in tables],
     )
     small = small.reshape(hidden, 2 * hidden)
-    at = hidden + features_used
+    shape = jax.ShapeDtypeStruct
+    results = pl.pallas_call(
+        functools.partial(finish_kernel, features_used),
+        out_shape=[shape((model_width, tok_dev), bf16)] * 3
+        + [
+            shape((2 * channels, hidden), f32),
+            shape((features_used, hidden), f32),
+            shape((1, hidden), f32),
+            shape((hidden, hidden), f32),
+            shape((1, hidden), f32),
+        ],
+        in_specs=[anywhere] * 4 + [vmem],
+        out_specs=[hbm] * 4 + [pl.BlockSpec()] * 4,
+        scratch_shapes=[dma((4,))],
+    )(value_out, first_out, second_out, weight_out, small)
     return (
-        value_out,
-        first_out,
-        second_out,
-        small[:, hidden:at],
-        small[:, at],
-        small[:, :hidden],
-        small[:, at + 1],
-        weight_out,
+        results[0],
+        results[1],
+        results[2],
+        results[4].T,
+        results[5].reshape(hidden),
+        results[6],
+        results[7].reshape(hidden),
+        results[3],
     )
 
 

time: 56 us -> 71 us (1.27)
  Pallas kernels: 39.7 us -> 53 us
  local copies, waits for them, and re-layouts: 15.2 us -> 16.7 us
    pallas_call x0 -> x1, Pallas kernels: none -> 15.4 us  [on_device(): pl.pallas_call(functools.partial(finish_kernel, features_used), out_shape...]
    unnamed x38 -> x44, local copies, waits for them, and re-layouts: 14.4 us -> 16.7 us
    pallas_call x1, Pallas kernels: 39.7 us -> 37.6 us  [on_device(): pl.pallas_call(functools.partial(operator_kernel, devices, channels, feat...]
    slice x2 -> x0, local copies, waits for them, and re-layouts: 0.77 us -> none  [the longest x1 0.7 us: on_device(): small[:, at + 1]]
where the time goes in v2:
time: 71 us; the launch traced here: 70.4 us
  Pallas kernels  53 us (75%)
  local copies, waits for them, and re-layouts  16.7 us (24%)
    pallas_call x1, Pallas kernels, on_device(): pl.pallas_call(functools.partial(operator_kernel, devices, channels, feat...  37.6 us
    unnamed x44, local copies, waits for them, and re-layouts  16.7 us
    pallas_call x1, Pallas kernels, on_device(): pl.pallas_call(functools.partial(finish_kernel, features_used), out_shape...  15.4 us

profile of v2, /device:TPU:0, one launch (start us, length us, event | category | flops | bytes accessed | tf_op | source)
XLA Modules:
  0.0 70.4 jit_solution(5015946488371109089)
XLA Ops:
  0.6 0.0 copy-start.19
  0.6 0.0 copy-start.20
  0.7 0.7 copy-done.19
  1.3 1.0 %copy-done = bf16[128,2048]{1,0:T(8,128)(2,1)S(1)} copy-done((bf16[128,2048]{1,0:T(8,128)(2,1)S(1)}, bf16[128,2048]{1,0:T(8,128)(2,1)}, u32[]{:S(2)}) %copy-start) | copy-done | bytes 524312
  2.4 1.0 %copy-done.1 = bf16[256,1024]{1,0:T(8,128)(2,1)S(1)} copy-done((bf16[256,1024]{1,0:T(8,128)(2,1)S(1)}, bf16[256,1024]{1,0:T(8,128)(2,1)}, u32[]{:S(2)}) %copy-start.1) | copy-done | bytes 524312
  3.4 1.0 %copy-done.2 = bf16[1024,256]{1,0:T(8,128)(2,1)S(1)} copy-done((bf16[1024,256]{1,0:T(8,128)(2,1)S(1)}, bf16[1024,256]{1,0:T(8,128)(2,1)}, u32[]{:S(2)}) %copy-start.2) | copy-done | bytes 524312
  4.5 0.9 %copy-done.3 = f32[1024,64]{0,1:T(8,128)S(1)} copy-done((f32[1024,64]{0,1:T(8,128)S(1)}, f32[1024,64]{0,1:T(8,128)}, u32[]{:S(2)}) %copy-start.3) | copy-done | bytes 262168
  5.4 0.9 %copy-done.4 = f32[512,128]{1,0:T(8,128)S(1)} copy-done((f32[512,128]{1,0:T(8,128)S(1)}, f32[512,128]{1,0:T(8,128)}, u32[]{:S(2)}) %copy-start.4) | copy-done | bytes 262168
  6.4 0.9 %copy-done.5 = f32[512,128]{1,0:T(8,128)S(1)} copy-done((f32[512,128]{1,0:T(8,128)S(1)}, f32[512,128]{1,0:T(8,128)}, u32[]{:S(2)}) %copy-start.5) | copy-done | bytes 262168
  7.3 0.9 %copy-done.6 = bf16[512,128]{1,0:T(8,128)(2,1)S(1)} copy-done((bf16[512,128]{1,0:T(8,128)(2,1)S(1)}, bf16[512,128]{1,0:T(8,128)(2,1)}, u32[]{:S(2)}) %copy-start.6) | copy-done | bytes 131096
  8.2 0.9 %copy-done.7 = bf16[512,128]{1,0:T(8,128)(2,1)S(1)} copy-done((bf16[512,128]{1,0:T(8,128)(2,1)S(1)}, bf16[512,128]{1,0:T(8,128)(2,1)}, u32[]{:S(2)}) %copy-start.7) | copy-done | bytes 131096
  9.1 0.9 %copy-done.8 = bf16[512,128]{1,0:T(8,128)(2,1)S(1)} copy-done((bf16[512,128]{1,0:T(8,128)(2,1)S(1)}, bf16[512,128]{1,0:T(8,128)(2,1)}, u32[]{:S(2)}) %copy-start.8) | copy-done | bytes 131096
  10.0 0.9 %copy-done.9 = bf16[512,128]{1,0:T(8,128)(2,1)S(1)} copy-done((bf16[512,128]{1,0:T(8,128)(2,1)S(1)}, bf16[512,128]{1,0:T(8,128)(2,1)}, u32[]{:S(2)}) %copy-start.9) | copy-done | bytes 131096
  10.9 0.9 %copy-done.13 = bf16[256,256]{1,0:T(8,128)(2,1)S(1)} copy-done((bf16[256,256]{1,0:T(8,128)(2,1)S(1)}, bf16[256,256]{1,0:T(8,128)(2,1)}, u32[]{:S(2)}) %copy-start.13) | copy-done | bytes 131096
  11.8 0.9 %copy-done.14 = bf16[256,256]{1,0:T(8,128)(2,1)S(1)} copy-done((bf16[256,256]{1,0:T(8,128)(2,1)S(1)}, bf16[256,256]{1,0:T(8,128)(2,1)}, u32[]{:S(2)}) %copy-start.14) | copy-done | bytes 131096
  12.7 0.8 %copy-done.15 = f32[64,64]{1,0:T(8,128)S(1)} copy-done((f32[64,64]{1,0:T(8,128)S(1)}, f32[64,64]{1,0:T(8,128)}, u32[]{:S(2)}) %copy-start.15) | copy-done | bytes 16408
  13.5 0.7 %copy-done.18 = f32[64,33]{0,1:T(8,128)S(1)} copy-done((f32[64,33]{0,1:T(8,128)S(1)}, f32[64,33]{0,1:T(8,128)}, u32[]{:S(2)}) %copy-start.18) | copy-done | bytes 8472
  14.2 37.6 %shard_map.224 = (bf16[512,128]{1,0:T(8,128)(2,1)S(1)}, bf16[512,128]{1,0:T(8,128)(2,1)S(1)}, bf16[512,128]{1,0:T(8,128)(2,1)S(1)}, f32[64,64]{1,0:T(8,128)S(1)}, f32[16,4,128]{2,1,0:T(4,128)S(1)}) custom-call(bf16[512,128]{1,0:T(8,128)(2,1)S(1)} %copy-done.6, bf16[512,128]{1,0:T(8,128)(2,1)S(1)} %copy-done.7, bf16[512,128]{1,0:T(8,128)(2,1)S(1)} %copy-done.8, ...), custom_call_target="tpu_custom_call" | custom-call | tf_op jit(solution)/shard_map/pallas_call | solution.py:724
  51.8 0.6 copy-done.10
  52.4 0.6 copy-done.11
  53.1 0.6 copy-done.12
  53.7 0.6 copy-done.16
  54.3 0.6 copy-done.17
  54.9 15.4 %shard_map.225 = (bf16[512,128]{1,0:T(8,128)(2,1)}, bf16[512,128]{1,0:T(8,128)(2,1)}, bf16[512,128]{1,0:T(8,128)(2,1)}, f32[64,64]{1,0:T(8,128)}, f32[33,64]{1,0...) custom-call(bf16[512,128]{1,0:T(8,128)(2,1)} %copy-done.10, bf16[512,128]{1,0:T(8,128)(2,1)} %copy-done.11, ...), custom_call_target="tpu_custom_call" | custom-call | tf_op jit(solution)/shard_map/pallas_call | solution.py:776
  (22 shorter events, 0.0 us)
Async XLA Ops:
  0.6 0.7 copy-start.19
  0.6 0.7 copy-start.20
  0.7 0.7 copy-start.21
  1.3 1.0 %copy-start = (bf16[128,2048]{1,0:T(8,128)(2,1)S(1)}, bf16[128,2048]{1,0:T(8,128)(2,1)}, u32[]{:S(2)}) copy-start(bf16[128,2048]{1,0:T(8,128)(2,1)} %constant.20.clone.features_hbm) | copy-start | bytes 1572868
  2.4 1.0 %copy-start.1 = (bf16[256,1024]{1,0:T(8,128)(2,1)S(1)}, bf16[256,1024]{1,0:T(8,128)(2,1)}, u32[]{:S(2)}) copy-start(bf16[256,1024]{1,0:T(8,128)(2,1)} %constant.15.clone.left_inv_hbm) | copy-start | bytes 1572868
  3.4 1.0 %copy-start.2 = (bf16[1024,256]{1,0:T(8,128)(2,1)S(1)}, bf16[1024,256]{1,0:T(8,128)(2,1)}, u32[]{:S(2)}) copy-start(bf16[1024,256]{1,0:T(8,128)(2,1)} %constant.14.clone.left_fwd_hbm) | copy-start | bytes 1572868
  4.5 0.9 %copy-start.3 = (f32[1024,64]{0,1:T(8,128)S(1)}, f32[1024,64]{0,1:T(8,128)}, u32[]{:S(2)}) copy-start(f32[1024,64]{0,1:T(8,128)} %param.25) | copy-start | bytes 786436
  5.4 0.9 %copy-start.4 = (f32[512,128]{1,0:T(8,128)S(1)}, f32[512,128]{1,0:T(8,128)}, u32[]{:S(2)}) copy-start(f32[512,128]{1,0:T(8,128)} %constant.19.clone.twid_sin_hbm) | copy-start | bytes 786436
  6.4 0.9 %copy-start.5 = (f32[512,128]{1,0:T(8,128)S(1)}, f32[512,128]{1,0:T(8,128)}, u32[]{:S(2)}) copy-start(f32[512,128]{1,0:T(8,128)} %constant.18.clone.twid_cos_hbm) | copy-start | bytes 786436
  7.3 0.9 %copy-start.6 = (bf16[512,128]{1,0:T(8,128)(2,1)S(1)}, bf16[512,128]{1,0:T(8,128)(2,1)}, u32[]{:S(2)}) copy-start(bf16[512,128]{1,0:T(8,128)(2,1)} %value_ref.1) | copy-start | bytes 393220
  8.2 0.9 %copy-start.7 = (bf16[512,128]{1,0:T(8,128)(2,1)S(1)}, bf16[512,128]{1,0:T(8,128)(2,1)}, u32[]{:S(2)}) copy-start(bf16[512,128]{1,0:T(8,128)(2,1)} %first_ref.1) | copy-start | bytes 393220
  9.1 0.9 %copy-start.8 = (bf16[512,128]{1,0:T(8,128)(2,1)S(1)}, bf16[512,128]{1,0:T(8,128)(2,1)}, u32[]{:S(2)}) copy-start(bf16[512,128]{1,0:T(8,128)(2,1)} %second_ref.1) | copy-start | bytes 393220
  10.0 0.9 %copy-start.9 = (bf16[512,128]{1,0:T(8,128)(2,1)S(1)}, bf16[512,128]{1,0:T(8,128)(2,1)}, u32[]{:S(2)}) copy-start(bf16[512,128]{1,0:T(8,128)(2,1)} %cot_ref.1) | copy-start | bytes 393220
  10.9 0.9 %copy-start.13 = (bf16[256,256]{1,0:T(8,128)(2,1)S(1)}, bf16[256,256]{1,0:T(8,128)(2,1)}, u32[]{:S(2)}) copy-start(bf16[256,256]{1,0:T(8,128)(2,1)} %constant.17.clone.right_inv_hbm) | copy-start | bytes 393220
  11.8 0.9 %copy-start.14 = (bf16[256,256]{1,0:T(8,128)(2,1)S(1)}, bf16[256,256]{1,0:T(8,128)(2,1)}, u32[]{:S(2)}) copy-start(bf16[256,256]{1,0:T(8,128)(2,1)} %constant.16.clone.right_fwd_hbm) | copy-start | bytes 393220
  12.7 0.8 %copy-start.15 = (f32[64,64]{1,0:T(8,128)S(1)}, f32[64,64]{1,0:T(8,128)}, u32[]{:S(2)}) copy-start(f32[64,64]{1,0:T(8,128)} %mid_weight_hbm.1) | copy-start | bytes 49156
  13.5 0.7 %copy-start.18 = (f32[64,33]{0,1:T(8,128)S(1)}, f32[64,33]{0,1:T(8,128)}, u32[]{:S(2)}) copy-start(f32[64,33]{0,1:T(8,128)} %param.21) | copy-start | bytes 25348
  51.8 0.7 copy-start.10
  52.4 0.7 copy-start.11
  53.1 0.6 copy-start.12
  53.7 0.6 copy-start.16
  54.3 0.6 copy-start.17

commit v3 on v2

--- a/solution.py
+++ b/solution.py
@@ -640,7 +640,7 @@
     first_in,
     second_in,
     weight_in,
-    small_ref,
+    small_in,
     value_out,
     first_out,
     second_out,
@@ -649,21 +649,29 @@
     pos_bias_out,
     mid_weight_out,
     mid_bias_out,
-    sem,
+    value_ref,
+    first_ref,
+    second_ref,
+    weight_ref,
+    small_ref,
+    in_sem,
+    out_sem,
 ):
-    copies = [
-        pltpu.make_async_copy(source, target, sem.at[at])
-        for at, (source, target) in enumerate(
-            (
-                (value_in, value_out),
-                (first_in, first_out),
-                (second_in, second_out),
-                (weight_in, weight_out),
-            )
-        )
+    sources = (small_in, value_in, first_in, second_in, weight_in)
+    held = (small_ref, value_ref, first_ref, second_ref, weight_ref)
+    targets = (None, value_out, first_out, second_out, weight_out)
+    loads = [
+        pltpu.make_async_copy(sources[at], held[at], in_sem.at[at]) for at in range(5)
     ]
-    for copy in copies:
-        copy.start()
+    stores = [
+        pltpu.make_async_copy(held[at], targets[at], out_sem.at[at]) for at in range(1, 5)
+    ]
+    for load in loads:
+        load.start()
+    for load, store in zip(loads[1:], stores):
+        load.wait()
+        store.start()
+    loads[0].wait()
     small = small_ref[...]
     turned = small.T
     last = 64 + features_used
@@ -671,8 +679,8 @@
     pos_bias_out[...] = turned[last : last + 1]
     mid_bias_out[...] = turned[last + 1 : last + 2]
     mid_weight_out[...] = small[:, :64]
-    for copy in copies:
-        copy.wait()
+    for store in stores:
+        store.wait()
 
 
 def on_device(
@@ -719,7 +727,6 @@
     dma = pltpu.SemaphoreType.DMA
     vmem = pl.BlockSpec(memory_space=pltpu.VMEM)
     hbm = pl.BlockSpec(memory_space=pltpu.HBM)
-    anywhere = pl.BlockSpec(memory_space=pl.ANY)
     bf16, f32 = jnp.bfloat16, jnp.float32
     value_out, first_out, second_out, weight_out, small = pl.pallas_call(
         functools.partial(operator_kernel, devices, channels, features_used),
@@ -756,7 +763,7 @@
             dma((4,)),
         ],
         compiler_params=pltpu.CompilerParams(
-            collective_id=0, has_side_effects=True, vmem_limit_bytes=50 * 1024 * 1024
+            collective_id=0, has_side_effects=True, vmem_limit_bytes=62 * 1024 * 1024
         ),
     )(
         value_branch,
@@ -783,9 +790,16 @@
             shape((hidden, hidden), f32),
             shape((1, hidden), f32),
         ],
-        in_specs=[anywhere] * 4 + [vmem],
+        in_specs=[hbm] * 5,
         out_specs=[hbm] * 4 + [pl.BlockSpec()] * 4,
-        scratch_shapes=[dma((4,))],
+        scratch_shapes=[pltpu.VMEM((model_width, tok_dev), bf16)] * 3
+        + [
+            pltpu.VMEM((2 * channels, hidden), f32),
+            pltpu.VMEM((hidden, 2 * hidden), f32),
+            dma((5,)),
+            dma((5,)),
+        ],
+        compiler_params=pltpu.CompilerParams(vmem_limit_bytes=62 * 1024 * 1024),
     )(value_out, first_out, second_out, weight_out, small)
     return (
         results[0],

time: 71 us -> 41.7 us (0.59)
  local copies, waits for them, and re-layouts: 16.7 us -> 0 us
  Pallas kernels: 53 us -> 40.9 us
    unnamed x44 -> x0, local copies, waits for them, and re-layouts: 16.7 us -> none
    pallas_call x1, Pallas kernels: 15.4 us -> 2.42 us  [on_device(): pl.pallas_call(functools.partial(finish_kernel, features_used), out_shape...]
    pallas_call x1, Pallas kernels: 37.6 us -> 38.5 us  [on_device(): pl.pallas_call(functools.partial(operator_kernel, devices, channels, feat...]
where the time goes in v3:
time: 41.7 us; the launch traced here: 41.5 us
  Pallas kernels  40.9 us (98%)
  between operations  0.64 us (2%)
    pallas_call x1, Pallas kernels, on_device(): pl.pallas_call(functools.partial(operator_kernel, devices, channels, feat...  38.5 us
    pallas_call x1, Pallas kernels, on_device(): pl.pallas_call(functools.partial(finish_kernel, features_used), out_shape...  2.42 us

profile of v3, /device:TPU:0, one launch (start us, length us, event | category | flops | bytes accessed | tf_op | source)
XLA Modules:
  0.0 41.5 jit_solution(8801586045917676385)
XLA Ops:
  0.6 38.5 %shard_map.224 = (bf16[512,128]{1,0:T(8,128)(2,1)}, bf16[512,128]{1,0:T(8,128)(2,1)}, bf16[512,128]{1,0:T(8,128)(2,1)}, f32[64,64]{1,0:T(8,128)}, f32[16,4,128]{2,1,0:T(4,128)}) custom-call(bf16[512,128]{1,0:T(8,128)(2,1)} %value_ref.1, bf16[512,128]{1,0:T(8,128)(2,1)} %first_ref.1, bf16[512,128]{1,0:T(8,128)(2,1)} %second_ref.1, bf16[512,128]{1,0:T(8,128)(2,1)} %cot_ref.1, ...), custom_call_target="tpu_custom_call" | custom-call | tf_op jit(solution)/shard_map/pallas_call | solution.py:731
  39.1 2.4 %shard_map.225 = (bf16[512,128]{1,0:T(8,128)(2,1)}, bf16[512,128]{1,0:T(8,128)(2,1)}, bf16[512,128]{1,0:T(8,128)(2,1)}, f32[64,64]{1,0:T(8,128)}, f32[33,64]{1,0...) custom-call(bf16[512,128]{1,0:T(8,128)(2,1)} %get-tuple-element.21.value_in, ...), custom_call_target="tpu_custom_call" | custom-call | tf_op jit(solution)/shard_map/pallas_call | solution.py:783

commit v4 on v3

--- a/solution.py
+++ b/solution.py
@@ -462,7 +462,7 @@
 
         lax.fori_loop(1, n, body, 0)
 
-    for at in range(4):
+    for at in range(2):
         for_peers(lambda peer, at=at: in_copy(at, peer, me).start())
 
     pos_table[...] = jnp.zeros_like(pos_table)
@@ -496,6 +496,8 @@
     ramp = lax.broadcasted_iota(jnp.int32, (1, seq_len), 1).astype(f32) * (1.0 / seq_len)
     window = jnp.exp(-own_rates * ramp)
     filters = (split_dot(own_weight, act_two) * window).astype(bf16)
+    for at in range(2, 4):
+        for_peers(lambda peer, at=at: in_copy(at, peer, me).start())
     for load in loads[7:]:
         load.wait()
 
@@ -616,6 +618,11 @@
             channels * o : channels * (o + 1)
         ]
 
+    for at in range(4):
+        for_peers(lambda peer, at=at: in_copy(at, peer, me).wait_send())
+    for at in range(2):
+        for_peers(lambda peer, at=at: out_copy(at, peer, me).wait_send())
+        for_peers(lambda peer, at=at: out_copy(at, peer, peer).wait_recv())
     for_peers(lambda peer: part_copy(peer, peer).wait_recv())
     total = small_recv[0]
     for at in range(1, n):
@@ -624,11 +631,8 @@
     small_out[me] = total
     for_peers(lambda peer: sum_copy(peer, me).start())
 
-    for at in range(4):
-        for_peers(lambda peer, at=at: in_copy(at, peer, me).wait_send())
-    for at in range(3):
-        for_peers(lambda peer, at=at: out_copy(at, peer, me).wait_send())
-        for_peers(lambda peer, at=at: out_copy(at, peer, peer).wait_recv())
+    for_peers(lambda peer: out_copy(2, peer, me).wait_send())
+    for_peers(lambda peer: out_copy(2, peer, peer).wait_recv())
     for_peers(lambda peer: part_copy(peer, me).wait_send())
     for_peers(lambda peer: sum_copy(peer, me).wait_send())
     for_peers(lambda peer: sum_copy(peer, peer).wait_recv())

time: 41.7 us -> 41.7 us (level)
  no operation moved by 1% of the time
where the time goes in v4:
time: 41.7 us; the launch traced here: 41.5 us
  Pallas kernels  40.9 us (98%)
  between operations  0.64 us (2%)
    pallas_call x1, Pallas kernels, on_device(): pl.pallas_call(functools.partial(operator_kernel, devices, channels, feat...  38.5 us
    pallas_call x1, Pallas kernels, on_device(): pl.pallas_call(functools.partial(finish_kernel, features_used), out_shape...  2.42 us

profile of v4, /device:TPU:0, one launch (start us, length us, event | category | flops | bytes accessed | tf_op | source)
XLA Modules:
  0.0 41.5 jit_solution(16694636427059451643)
XLA Ops:
  0.6 38.5 %shard_map.224 = (bf16[512,128]{1,0:T(8,128)(2,1)}, bf16[512,128]{1,0:T(8,128)(2,1)}, bf16[512,128]{1,0:T(8,128)(2,1)}, f32[64,64]{1,0:T(8,128)}, f32[16,4,128]{2,1,0:T(4,128)}) custom-call(bf16[512,128]{1,0:T(8,128)(2,1)} %value_ref.1, bf16[512,128]{1,0:T(8,128)(2,1)} %first_ref.1, bf16[512,128]{1,0:T(8,128)(2,1)} %second_ref.1, bf16[512,128]{1,0:T(8,128)(2,1)} %cot_ref.1, ...), custom_call_target="tpu_custom_call" | custom-call | tf_op jit(solution)/shard_map/pallas_call | solution.py:735
  39.1 2.4 %shard_map.225 = (bf16[512,128]{1,0:T(8,128)(2,1)}, bf16[512,128]{1,0:T(8,128)(2,1)}, bf16[512,128]{1,0:T(8,128)(2,1)}, f32[64,64]{1,0:T(8,128)}, f32[33,64]{1,0...) custom-call(bf16[512,128]{1,0:T(8,128)(2,1)} %get-tuple-element.21.value_in, ...), custom_call_target="tpu_custom_call" | custom-call | tf_op jit(solution)/shard_map/pallas_call | solution.py:787

commit v5 on v4

--- a/solution.py
+++ b/solution.py
@@ -379,7 +379,7 @@
 
     lax.fori_loop(1, n, greet, 0)
 
-    inputs = (value_ref, first_ref, cot_ref, second_ref)
+    inputs = (cot_ref, second_ref, first_ref, value_ref)
     own_rows = pl.ds(pl.multiple_of(me * channels, channels), channels)
     pair = lax.rem(me, 2)
     column = me // 2
@@ -577,19 +577,19 @@
 
     spec_one = forward(to_sections(filters[:channels]))
     spec_two = forward(to_sections(filters[channels:]))
-    spec_val = forward(arrived(0))
+    cot = arrived(0).astype(f32)
+    second = arrived(1).astype(f32)
+    spec_gtwo = forward((cot * second).astype(bf16))
+    gated_grad = inverse(spec_two, spec_gtwo, True, False)
+    first = arrived(2).astype(f32)
+    spec_gone = forward((gated_grad * first).astype(bf16))
+    send_out(2, inverse(spec_one, spec_gone, True, False).astype(bf16))
+    spec_val = forward(arrived(3))
     conv_one = inverse(spec_one, spec_val, False, False)
-    first = arrived(1).astype(f32)
+    send_out(1, (gated_grad * conv_one).astype(bf16))
     spec_gated = forward((first * conv_one).astype(bf16))
     conv_two = inverse(spec_two, spec_gated, False, False)
-    cot = arrived(2).astype(f32)
     send_out(0, (cot * conv_two).astype(bf16))
-    second = arrived(3).astype(f32)
-    spec_gtwo = forward((cot * second).astype(bf16))
-    gated_grad = inverse(spec_two, spec_gtwo, True, False)
-    send_out(1, (gated_grad * conv_one).astype(bf16))
-    spec_gone = forward((gated_grad * first).astype(bf16))
-    send_out(2, inverse(spec_one, spec_gone, True, False).astype(bf16))
     filt_one = from_sections(inverse(spec_gone, spec_val, False, True))
     filt_two = from_sections(inverse(spec_gtwo, spec_gated, False, True))
     filter_grad = jnp.concatenate([filt_one, filt_two], axis=0) * window * (1.0 / seq_len)

time: 41.7 us -> 42.9 us (1.029)
  Pallas kernels: 40.9 us -> 42.1 us
    pallas_call x1, Pallas kernels: 38.5 us -> 39.7 us  [on_device(): pl.pallas_call(functools.partial(operator_kernel, devices, channels, feat...]
where the time goes in v5:
time: 42.9 us; the launch traced here: 42.7 us
  Pallas kernels  42.1 us (98%)
  between operations  0.64 us (1%)
    pallas_call x1, Pallas kernels, on_device(): pl.pallas_call(functools.partial(operator_kernel, devices, channels, feat...  39.7 us
    pallas_call x1, Pallas kernels, on_device(): pl.pallas_call(functools.partial(finish_kernel, features_used), out_shape...  2.42 us

profile of v5, /device:TPU:0, one launch (start us, length us, event | category | flops | bytes accessed | tf_op | source)
XLA Modules:
  0.0 42.7 jit_solution(11325550346564468599)
XLA Ops:
  0.6 39.7 %shard_map.224 = (bf16[512,128]{1,0:T(8,128)(2,1)}, bf16[512,128]{1,0:T(8,128)(2,1)}, bf16[512,128]{1,0:T(8,128)(2,1)}, f32[64,64]{1,0:T(8,128)}, f32[16,4,128]{2,1,0:T(4,128)}) custom-call(bf16[512,128]{1,0:T(8,128)(2,1)} %value_ref.1, bf16[512,128]{1,0:T(8,128)(2,1)} %first_ref.1, bf16[512,128]{1,0:T(8,128)(2,1)} %second_ref.1, bf16[512,128]{1,0:T(8,128)(2,1)} %cot_ref.1, ...), custom_call_target="tpu_custom_call" | custom-call | tf_op jit(solution)/shard_map/pallas_call | solution.py:735
  40.3 2.4 %shard_map.225 = (bf16[512,128]{1,0:T(8,128)(2,1)}, bf16[512,128]{1,0:T(8,128)(2,1)}, bf16[512,128]{1,0:T(8,128)(2,1)}, f32[64,64]{1,0:T(8,128)}, f32[33,64]{1,0...) custom-call(bf16[512,128]{1,0:T(8,128)(2,1)} %get-tuple-element.21.value_in, ...), custom_call_target="tpu_custom_call" | custom-call | tf_op jit(solution)/shard_map/pallas_call | solution.py:787
